TPU v7x, 128 devices: a whole 4x4x4 slice. The times are simulated.
128 devices in a mesh: blk: 16 (over x_lo, z, core), head: 8 (over x_hi, y).
Axes of the slice: x: 4 (x_hi: 2, x_lo: 2; x = x_hi * 2 + x_lo), y: 4, z: 4, core: 2. Of those that a mesh axis runs over, the one named last changes fastest.
Arguments:
- queries: bfloat16 [32768, 2048], P(('blk', 'head')), may hold values from -10 to 10
- keys: bfloat16 [32768, 2048], P(('blk', 'head')), may hold values from -3 to 3
- values: bfloat16 [32768, 2048], P(('blk', 'head')), may hold values from -6 to 6
- active: int32 [256, 24], replicated, may hold values from 0 to 255, as said below
Outputs:
- attended: bfloat16 [32768, 2048], P(('blk', 'head'))
Inputs may be any that keep to these rules, and one draw needn't show every extreme that they name: `active`: row b lists 24 different key blocks; its first entry is b itself.
All inputs are finite; a program needn't handle non-finite values.
Results may differ from a plain program's by a relative error of at most 0.0047.
Values may be sent and summed in bfloat16 or wider, within the bound.
No kernel may reach another device: no remote copies, remote signals or barrier semaphores. Data moves between devices by JAX's collectives and lax.ppermute only.
A program may use at most 256 MiB of HBM per device.

v0:
```python
import math

import jax
import jax.numpy as jnp
from jax import lax
from jax.sharding import PartitionSpec as P

HD = 64
BLOCK = 128
ACT = 24


def attend_all(q_loc, k_all, v_all, key_rows):
    rows_loc = q_loc.shape[0]
    width = q_loc.shape[1]
    heads = width // HD
    blocks = rows_loc // BLOCK
    blocks_all = k_all.shape[0] // BLOCK
    scale = 1.0 / math.sqrt(HD)
    group = math.gcd(blocks, max(1, 512 // BLOCK))
    count_g = blocks // group
    k_view = k_all.reshape(blocks_all, BLOCK, heads, HD)
    v_view = v_all.reshape(blocks_all, BLOCK, heads, HD)
    q_groups = q_loc.reshape(count_g, group, BLOCK, heads, HD)
    block_ids = (key_rows // BLOCK).reshape(count_g, group * ACT)

    def one_group(args):
        q_blk, listed = args
        shape = (group, ACT, BLOCK, heads, HD)
        k_sel = jnp.take(k_view, listed, axis=0).reshape(shape)
        v_sel = jnp.take(v_view, listed, axis=0).reshape(shape)
        scores = (
            jnp.einsum("gqhd,gakhd->ghqak", q_blk, k_sel, preferred_element_type=jnp.float32)
            * scale
        )
        top = jnp.max(scores, axis=(3, 4), keepdims=True)
        weights = jnp.exp(scores - top)
        total = jnp.sum(weights, axis=(3, 4))
        product = jnp.einsum(
            "ghqak,gakhd->gqhd",
            weights.astype(jnp.bfloat16),
            v_sel,
            preferred_element_type=jnp.float32,
        )
        return (product / jnp.transpose(total, (0, 2, 1))[..., None]).astype(jnp.bfloat16)

    result = lax.map(one_group, (q_groups, block_ids))
    return result.reshape(rows_loc, width)


def listed_rows(active, shards, tok, regrouped_rows):
    per_shard = tok // BLOCK
    query_ids = (
        shards[:, None] * per_shard + jnp.arange(per_shard, dtype=jnp.int32)[None, :]
    ).reshape(-1)
    key_ids = jnp.take(active, query_ids, axis=0)
    return regrouped_rows(key_ids * BLOCK)


def on_device(queries, keys, values, active):
    tok = queries.shape[0]
    n_head = lax.axis_size("head")
    q_loc, k_loc, v_loc = (
        lax.all_to_all(queries, "head", split_axis=1, concat_axis=0, tiled=True),
        lax.all_to_all(keys, "head", split_axis=1, concat_axis=0, tiled=True),
        lax.all_to_all(values, "head", split_axis=1, concat_axis=0, tiled=True),
    )
    sources = q_loc.shape[0] // tok
    shards = lax.axis_index("blk") * n_head + jnp.arange(sources, dtype=jnp.int32)

    def direct_rows(first_token):
        return first_token

    key_rows = listed_rows(active, shards, tok, direct_rows)
    k_all, v_all = (
        lax.all_gather(k_loc, "blk", axis=0, tiled=True),
        lax.all_gather(v_loc, "blk", axis=0, tiled=True),
    )
    mixed = attend_all(q_loc, k_all, v_all, key_rows)
    return lax.all_to_all(mixed, "head", split_axis=0, concat_axis=1, tiled=True)


def solution(mesh):
    in_specs = (P(("blk", "head"), None), P(("blk", "head"), None), P(("blk", "head"), None), P())
    out_specs = P(("blk", "head"), None)
    return jax.shard_map(
        on_device, mesh=mesh, in_specs=in_specs, out_specs=out_specs, check_vma=False
    )
```

profile of v0, /device:TPU:6, one launch (start us, length us, event | category | flops | bytes accessed | tf_op | source)
XLA Modules:
  0.0 695.8 jit_solution(13654390739428253230)
XLA Ops:
  6.5 1.6 copy.63
  8.1 0.5 copy.64
  8.6 21.5 %all_to_all.73 = bf16[256,8,256]{2,0,1:T(8,128)(2,1)S(1)} all-to-all(bf16[256,8,256]{2,0,1:T(8,128)(2,1)S(1)} %copy.64), channel_id=1, replica_groups=mesh['blk'=16,'head'=8] {'head'}, dimensions={1} | all-to-all | bytes 2097152 | tf_op jit(solution)/shard_map/all_to_all | solution.py:66
  30.1 1.4 copy.65
  31.6 1.5 copy.68
  33.1 0.5 copy.69
  33.6 26.7 %all_to_all.74 = bf16[256,8,256]{2,0,1:T(8,128)(2,1)S(1)} all-to-all(bf16[256,8,256]{2,0,1:T(8,128)(2,1)S(1)} %copy.69), channel_id=1, replica_groups=mesh['blk'=16,'head'=8] {'head'}, dimensions={1} | all-to-all | bytes 2097152 | tf_op jit(solution)/shard_map/all_to_all | solution.py:65
  60.3 1.4 copy.70
  61.8 1.3 copy.66
  63.1 7.5 %all-to-all-start.1 = ((bf16[256,8,256]{0,2,1:T(8,128)(2,1)}), bf16[256,8,256]{0,2,1:T(8,128)(2,1)S(1)}, u32[]{:S(2)}, u32[]{:S(2)}) async-start(bf16[256,8,256]{0,2,1:T(8,128)(2,1)} %bitcast.17), calls=%async_computation.1 | async-start | bytes 2097152 | tf_op jit(solution)/shard_map/all_to_all | solution.py:64
  70.6 0.1 add.93
  70.7 0.1 copy.62
  70.8 0.6 gather_fusion.2
  71.4 0.1 gather.10
  71.5 0.1 add.85
  71.6 0.1 copy.60
  71.7 0.1 copy.61
  71.9 0.1 broadcast_in_dim.34
  72.0 19.7 %all-to-all-done.1 = bf16[256,8,256]{0,2,1:T(8,128)(2,1)S(1)} async-done(((bf16[256,8,256]{0,2,1:T(8,128)(2,1)}), bf16[256,8,256]{0,2,1:T(8,128)(2,1)S(1)}, u32[]{:S(2)}, u32[]{:S(2)}) %all-to-all-start.1) | async-done | bytes 1048608 | tf_op jit(solution)/shard_map/all_to_all | solution.py:64
  91.7 0.6 copy.67
  92.3 0.3 reshape.91
  92.6 49.5 %all-gather.3.cloned.1.call-done = bf16[32768,256]{0,1:T(8,128)(2,1)} async-done(((bf16[2048,256]{0,1:T(8,128)(2,1)}), bf16[32768,256]{0,1:T(8,128)(2,1)}) %all-gather.3.cloned.1.call-update) | async-done | bytes 16777232 | tf_op jit(solution)/shard_map/all_gather | solution.py:77
  142.1 15.2 %copy.83 = bf16[32,8,256,128]{3,2,1,0:T(8,128)(2,1)} copy(bf16[32,8,256,128]{3,1,2,0:T(8,128)(2,1)} %bitcast.76) | data formatting | bytes 33554432
  157.3 37.2 %copy.71 = bf16[256,128,4,64]{3,2,1,0:T(4,128)(2,1)} copy(bf16[256,128,4,64]{1,0,3,2:T(8,128)(2,1)} %bitcast.74) | data formatting | bytes 33554432 | tf_op jit(solution)/shard_map/while | solution.py:47
  194.5 43.3 %all-gather.5.cloned.1.call-done = bf16[32768,256]{0,1:T(8,128)(2,1)} async-done(((bf16[2048,256]{0,1:T(8,128)(2,1)}), bf16[32768,256]{0,1:T(8,128)(2,1)}) %all-gather.5.cloned.1.call-update) | async-done | bytes 16777232 | tf_op jit(solution)/shard_map/all_gather | solution.py:76
  237.8 15.1 %copy.84 = bf16[32,8,256,128]{3,2,1,0:T(8,128)(2,1)} copy(bf16[32,8,256,128]{3,1,2,0:T(8,128)(2,1)} %bitcast.77) | data formatting | bytes 33554432
  252.9 37.1 %copy.73 = bf16[256,128,4,64]{3,2,1,0:T(4,128)(2,1)} copy(bf16[256,128,4,64]{1,0,3,2:T(8,128)(2,1)} %bitcast.75) | data formatting | bytes 33554432 | tf_op jit(solution)/shard_map/while | solution.py:47
  289.9 375.0 %while.10 = (s32[]{:T(128)}, bf16[4,4,128,4,64]{2,1,0,4,3:T(4,128)(2,1)S(1)}, s32[4,96]{1,0:T(4,128)S(1)}, bf16[256,128,4,64]{3,2,1,0:T(4,128)(2,1)}, bf16[4,4,1...) while((s32[]{:T(128)}, bf16[4,4,128,4,64]{2,1,0,4,3:T(4,128)(2,1)S(1)}, ...), condition=%wide.region_3.5_spmd, body=%wide.region_0.4_spmd.sunk | while | flops 1667495424 | bytes 140032144 | solution.py:47
  290.0 14.7 %gather_fusion = bf16[96,128,4,64]{3,2,1,0:T(4,128)(2,1)} fusion(bf16[256,128,4,64]{3,2,1,0:T(4,128)(2,1)} %get-tuple-element.147, s32[1024]{0:T(1024)S(1)} %pad_clamp_fusion.3), kind=kCustom, calls=%fused_computation.clone.clone.1 | custom fusion | bytes 12583296 | tf_op jit(solution)/shard_map/while/body/eval_jaxpr/jit(_take)/gather | solution.py:31
  304.7 14.7 %gather_fusion.1 = bf16[96,128,4,64]{3,2,1,0:T(4,128)(2,1)} fusion(bf16[256,128,4,64]{3,2,1,0:T(4,128)(2,1)} %get-tuple-element.149, s32[1024]{0:T(1024)S(1)} %pad_clamp_fusion.3), kind=kCustom, calls=%fused_computation.1.clone.clone.1 | custom fusion | bytes 12583296 | tf_op jit(solution)/shard_map/while/body/eval_jaxpr/jit(_take)/gather | solution.py:30
  319.4 25.1 %broadcast_select_fusion.3 = (bf16[96,128,4,64]{3,2,1,0:T(4,128)(2,1)}, bf16[96,128,4,64]{3,2,1,0:T(4,128)(2,1)}) fusion(bf16[96,128,4,64]{3,2,1,0:T(4,128)(2,1)} %gather_fusion, pred[96]{0:T(512)(128)(4,1)S(1)} %get-tuple-element.125, bf16[96,128,4,64]{3,2,1,0:T(4,128)(2,1)} %gather_fusion.1), kind=kLoop, calls=%fused_computation.14.clone.1 | loop fusion | flops 6291456 | bytes 25165920 | tf_op jit(solution)/shard_map/while/body/eval_jaxpr/jit(_take)/select_n | solution.py:31
  344.5 0.1 constant_dynamic-slice_fusion.3
  344.6 12.8 %multiply_reduce_fusion.2 = (f32[4,4,128]{2,1,0:T(4,128)S(1)}, f32[4,4,128,24,128]{2,4,3,1,0:T(8,128)}) fusion(bf16[4,24,128,4,64]{4,3,2,1,0:T(4,128)(2,1)} %bitcast.72, bf16[1,4,128,4,64]{2,1,0,4,3:T(4,128)(2,1)S(1)} %constant_dynamic-slice_fusion.3), kind=kOutput, calls=%fused_computation.4.clone.1 | convolution fusion | flops 817887232 | bytes 31727616 | tf_op jit(solution)/shard_map/while/body/eval_jaxpr/gqhd,gakhd->ghqak/dot_general | solution.py:33
  357.5 10.4 %fusion.40 = f32[4,4,128]{2,1,0:T(4,128)S(1)} fusion(f32[4,4,128,24,128]{2,4,3,1,0:T(8,128)} %get-tuple-element.127, f32[4,4,128]{2,1,0:T(4,128)S(1)} %get-tuple-element.128), kind=kLoop, calls=%fused_computation.5.clone.1 | loop fusion | flops 18872320 | bytes 25182208 | tf_op jit(solution)/shard_map/while/body/eval_jaxpr/reduce_sum | solution.py:38
  367.9 15.5 %fusion.41 = bf16[1,4,128,4,64]{2,4,3,1,0:T(8,128)(2,1)S(1)} fusion(f32[4,4,128,24,128]{2,4,3,1,0:T(8,128)} %get-tuple-element.127, f32[4,4,128]{2,1,0:T(4,128)S(1)} %get-tuple-element.128, bf16[4,24,128,4,64]{4,3,2,1,0:T(4,128)(2,1)} %bitcast.73, f32[4,128,4]{1,2,0:T(4,128)S(1)} %bitcast.84), kind=kOutput, calls=%fused_computation.18.clone.1 | convolution fusion | flops 824442880 | bytes 31735808 | tf_op jit(solution)/shard_map/while/body/eval_jaxpr/ghqak,gakhd->gqhd/dot_general | solution.py:39
  383.4 0.3 copy_dynamic-update-slice_fusion.2
  383.7 14.7 %gather_fusion = bf16[96,128,4,64]{3,2,1,0:T(4,128)(2,1)} fusion(bf16[256,128,4,64]{3,2,1,0:T(4,128)(2,1)} %get-tuple-element.147, s32[1024]{0:T(1024)S(1)} %pad_clamp_fusion.3), kind=kCustom, calls=%fused_computation.clone.clone.1 | custom fusion | bytes 12583296 | tf_op jit(solution)/shard_map/while/body/eval_jaxpr/jit(_take)/gather | solution.py:31
  398.5 14.7 %gather_fusion.1 = bf16[96,128,4,64]{3,2,1,0:T(4,128)(2,1)} fusion(bf16[256,128,4,64]{3,2,1,0:T(4,128)(2,1)} %get-tuple-element.149, s32[1024]{0:T(1024)S(1)} %pad_clamp_fusion.3), kind=kCustom, calls=%fused_computation.1.clone.clone.1 | custom fusion | bytes 12583296 | tf_op jit(solution)/shard_map/while/body/eval_jaxpr/jit(_take)/gather | solution.py:30
  413.2 25.1 %broadcast_select_fusion.3 = (bf16[96,128,4,64]{3,2,1,0:T(4,128)(2,1)}, bf16[96,128,4,64]{3,2,1,0:T(4,128)(2,1)}) fusion(bf16[96,128,4,64]{3,2,1,0:T(4,128)(2,1)} %gather_fusion, pred[96]{0:T(512)(128)(4,1)S(1)} %get-tuple-element.125, bf16[96,128,4,64]{3,2,1,0:T(4,128)(2,1)} %gather_fusion.1), kind=kLoop, calls=%fused_computation.14.clone.1 | loop fusion | flops 6291456 | bytes 25165920 | tf_op jit(solution)/shard_map/while/body/eval_jaxpr/jit(_take)/select_n | solution.py:31
  438.3 0.1 constant_dynamic-slice_fusion.3
  438.4 12.8 %multiply_reduce_fusion.2 = (f32[4,4,128]{2,1,0:T(4,128)S(1)}, f32[4,4,128,24,128]{2,4,3,1,0:T(8,128)}) fusion(bf16[4,24,128,4,64]{4,3,2,1,0:T(4,128)(2,1)} %bitcast.72, bf16[1,4,128,4,64]{2,1,0,4,3:T(4,128)(2,1)S(1)} %constant_dynamic-slice_fusion.3), kind=kOutput, calls=%fused_computation.4.clone.1 | convolution fusion | flops 817887232 | bytes 31727616 | tf_op jit(solution)/shard_map/while/body/eval_jaxpr/gqhd,gakhd->ghqak/dot_general | solution.py:33
  451.2 10.4 %fusion.40 = f32[4,4,128]{2,1,0:T(4,128)S(1)} fusion(f32[4,4,128,24,128]{2,4,3,1,0:T(8,128)} %get-tuple-element.127, f32[4,4,128]{2,1,0:T(4,128)S(1)} %get-tuple-element.128), kind=kLoop, calls=%fused_computation.5.clone.1 | loop fusion | flops 18872320 | bytes 25182208 | tf_op jit(solution)/shard_map/while/body/eval_jaxpr/reduce_sum | solution.py:38
  461.7 15.5 %fusion.41 = bf16[1,4,128,4,64]{2,4,3,1,0:T(8,128)(2,1)S(1)} fusion(f32[4,4,128,24,128]{2,4,3,1,0:T(8,128)} %get-tuple-element.127, f32[4,4,128]{2,1,0:T(4,128)S(1)} %get-tuple-element.128, bf16[4,24,128,4,64]{4,3,2,1,0:T(4,128)(2,1)} %bitcast.73, f32[4,128,4]{1,2,0:T(4,128)S(1)} %bitcast.84), kind=kOutput, calls=%fused_computation.18.clone.1 | convolution fusion | flops 824442880 | bytes 31735808 | tf_op jit(solution)/shard_map/while/body/eval_jaxpr/ghqak,gakhd->gqhd/dot_general | solution.py:39
  477.1 0.3 copy_dynamic-update-slice_fusion.2
  477.5 14.7 %gather_fusion = bf16[96,128,4,64]{3,2,1,0:T(4,128)(2,1)} fusion(bf16[256,128,4,64]{3,2,1,0:T(4,128)(2,1)} %get-tuple-element.147, s32[1024]{0:T(1024)S(1)} %pad_clamp_fusion.3), kind=kCustom, calls=%fused_computation.clone.clone.1 | custom fusion | bytes 12583296 | tf_op jit(solution)/shard_map/while/body/eval_jaxpr/jit(_take)/gather | solution.py:31
  492.2 14.7 %gather_fusion.1 = bf16[96,128,4,64]{3,2,1,0:T(4,128)(2,1)} fusion(bf16[256,128,4,64]{3,2,1,0:T(4,128)(2,1)} %get-tuple-element.149, s32[1024]{0:T(1024)S(1)} %pad_clamp_fusion.3), kind=kCustom, calls=%fused_computation.1.clone.clone.1 | custom fusion | bytes 12583296 | tf_op jit(solution)/shard_map/while/body/eval_jaxpr/jit(_take)/gather | solution.py:30
  506.9 25.1 %broadcast_select_fusion.3 = (bf16[96,128,4,64]{3,2,1,0:T(4,128)(2,1)}, bf16[96,128,4,64]{3,2,1,0:T(4,128)(2,1)}) fusion(bf16[96,128,4,64]{3,2,1,0:T(4,128)(2,1)} %gather_fusion, pred[96]{0:T(512)(128)(4,1)S(1)} %get-tuple-element.125, bf16[96,128,4,64]{3,2,1,0:T(4,128)(2,1)} %gather_fusion.1), kind=kLoop, calls=%fused_computation.14.clone.1 | loop fusion | flops 6291456 | bytes 25165920 | tf_op jit(solution)/shard_map/while/body/eval_jaxpr/jit(_take)/select_n | solution.py:31
  532.0 0.1 constant_dynamic-slice_fusion.3
  532.1 12.8 %multiply_reduce_fusion.2 = (f32[4,4,128]{2,1,0:T(4,128)S(1)}, f32[4,4,128,24,128]{2,4,3,1,0:T(8,128)}) fusion(bf16[4,24,128,4,64]{4,3,2,1,0:T(4,128)(2,1)} %bitcast.72, bf16[1,4,128,4,64]{2,1,0,4,3:T(4,128)(2,1)S(1)} %constant_dynamic-slice_fusion.3), kind=kOutput, calls=%fused_computation.4.clone.1 | convolution fusion | flops 817887232 | bytes 31727616 | tf_op jit(solution)/shard_map/while/body/eval_jaxpr/gqhd,gakhd->ghqak/dot_general | solution.py:33
  545.0 10.4 %fusion.40 = f32[4,4,128]{2,1,0:T(4,128)S(1)} fusion(f32[4,4,128,24,128]{2,4,3,1,0:T(8,128)} %get-tuple-element.127, f32[4,4,128]{2,1,0:T(4,128)S(1)} %get-tuple-element.128), kind=kLoop, calls=%fused_computation.5.clone.1 | loop fusion | flops 18872320 | bytes 25182208 | tf_op jit(solution)/shard_map/while/body/eval_jaxpr/reduce_sum | solution.py:38
  555.4 15.5 %fusion.41 = bf16[1,4,128,4,64]{2,4,3,1,0:T(8,128)(2,1)S(1)} fusion(f32[4,4,128,24,128]{2,4,3,1,0:T(8,128)} %get-tuple-element.127, f32[4,4,128]{2,1,0:T(4,128)S(1)} %get-tuple-element.128, bf16[4,24,128,4,64]{4,3,2,1,0:T(4,128)(2,1)} %bitcast.73, f32[4,128,4]{1,2,0:T(4,128)S(1)} %bitcast.84), kind=kOutput, calls=%fused_computation.18.clone.1 | convolution fusion | flops 824442880 | bytes 31735808 | tf_op jit(solution)/shard_map/while/body/eval_jaxpr/ghqak,gakhd->gqhd/dot_general | solution.py:39
  570.9 0.3 copy_dynamic-update-slice_fusion.2
  571.2 14.7 %gather_fusion = bf16[96,128,4,64]{3,2,1,0:T(4,128)(2,1)} fusion(bf16[256,128,4,64]{3,2,1,0:T(4,128)(2,1)} %get-tuple-element.147, s32[1024]{0:T(1024)S(1)} %pad_clamp_fusion.3), kind=kCustom, calls=%fused_computation.clone.clone.1 | custom fusion | bytes 12583296 | tf_op jit(solution)/shard_map/while/body/eval_jaxpr/jit(_take)/gather | solution.py:31
  586.0 14.7 %gather_fusion.1 = bf16[96,128,4,64]{3,2,1,0:T(4,128)(2,1)} fusion(bf16[256,128,4,64]{3,2,1,0:T(4,128)(2,1)} %get-tuple-element.149, s32[1024]{0:T(1024)S(1)} %pad_clamp_fusion.3), kind=kCustom, calls=%fused_computation.1.clone.clone.1 | custom fusion | bytes 12583296 | tf_op jit(solution)/shard_map/while/body/eval_jaxpr/jit(_take)/gather | solution.py:30
  600.7 25.1 %broadcast_select_fusion.3 = (bf16[96,128,4,64]{3,2,1,0:T(4,128)(2,1)}, bf16[96,128,4,64]{3,2,1,0:T(4,128)(2,1)}) fusion(bf16[96,128,4,64]{3,2,1,0:T(4,128)(2,1)} %gather_fusion, pred[96]{0:T(512)(128)(4,1)S(1)} %get-tuple-element.125, bf16[96,128,4,64]{3,2,1,0:T(4,128)(2,1)} %gather_fusion.1), kind=kLoop, calls=%fused_computation.14.clone.1 | loop fusion | flops 6291456 | bytes 25165920 | tf_op jit(solution)/shard_map/while/body/eval_jaxpr/jit(_take)/select_n | solution.py:31
  625.8 0.1 constant_dynamic-slice_fusion.3
  625.9 12.8 %multiply_reduce_fusion.2 = (f32[4,4,128]{2,1,0:T(4,128)S(1)}, f32[4,4,128,24,128]{2,4,3,1,0:T(8,128)}) fusion(bf16[4,24,128,4,64]{4,3,2,1,0:T(4,128)(2,1)} %bitcast.72, bf16[1,4,128,4,64]{2,1,0,4,3:T(4,128)(2,1)S(1)} %constant_dynamic-slice_fusion.3), kind=kOutput, calls=%fused_computation.4.clone.1 | convolution fusion | flops 817887232 | bytes 31727616 | tf_op jit(solution)/shard_map/while/body/eval_jaxpr/gqhd,gakhd->ghqak/dot_general | solution.py:33
  638.7 10.4 %fusion.40 = f32[4,4,128]{2,1,0:T(4,128)S(1)} fusion(f32[4,4,128,24,128]{2,4,3,1,0:T(8,128)} %get-tuple-element.127, f32[4,4,128]{2,1,0:T(4,128)S(1)} %get-tuple-element.128), kind=kLoop, calls=%fused_computation.5.clone.1 | loop fusion | flops 18872320 | bytes 25182208 | tf_op jit(solution)/shard_map/while/body/eval_jaxpr/reduce_sum | solution.py:38
  649.2 15.5 %fusion.41 = bf16[1,4,128,4,64]{2,4,3,1,0:T(8,128)(2,1)S(1)} fusion(f32[4,4,128,24,128]{2,4,3,1,0:T(8,128)} %get-tuple-element.127, f32[4,4,128]{2,1,0:T(4,128)S(1)} %get-tuple-element.128, bf16[4,24,128,4,64]{4,3,2,1,0:T(4,128)(2,1)} %bitcast.73, f32[4,128,4]{1,2,0:T(4,128)S(1)} %bitcast.84), kind=kOutput, calls=%fused_computation.18.clone.1 | convolution fusion | flops 824442880 | bytes 31735808 | tf_op jit(solution)/shard_map/while/body/eval_jaxpr/ghqak,gakhd->gqhd/dot_general | solution.py:39
  664.6 0.3 copy_dynamic-update-slice_fusion.2
  664.9 0.7 all_to_all.65
  665.7 0.2 copy.75
  665.9 21.6 %all_to_all.75 = bf16[8,256,256]{1,2,0:T(8,128)(2,1)S(1)} all-to-all(bf16[8,256,256]{1,2,0:T(8,128)(2,1)S(1)} %copy.75), channel_id=1, replica_groups=mesh['blk'=16,'head'=8] {'head'}, dimensions={0} | all-to-all | bytes 2097152 | tf_op jit(solution)/shard_map/all_to_all | solution.py:80
  687.5 1.4 copy.76
  (27 shorter events, 0.4 us)
Async XLA Ops:
  6.5 55.2 %copy-start = (bf16[256,2048]{1,0:T(8,128)(2,1)S(1)}, bf16[256,2048]{1,0:T(8,128)(2,1)}, u32[]{:S(2)}) copy-start(bf16[256,2048]{1,0:T(8,128)(2,1)} %param.8) | copy-start | bytes 3145732
  6.5 64.2 %copy-start.1 = (s32[256,24]{0,1:T(8,128)S(1)}, s32[256,24]{0,1:T(8,128)}, u32[]{:S(2)}) copy-start(s32[256,24]{0,1:T(8,128)} %param.11) | copy-start | bytes 73732
  6.5 135.6 %all-gather.3.cloned.1.call-start = ((), (), s32[]{:S(2)}) async-start(), calls=%async_computation.4 | async-start | bytes 17825792 | tf_op jit(solution)/shard_map/all_gather | solution.py:77
  31.6 206.2 %all-gather.5.cloned.1.call-start = ((), (), s32[]{:S(2)}) async-start(), calls=%async_computation.5 | async-start | bytes 17825792 | tf_op jit(solution)/shard_map/all_gather | solution.py:76
  63.1 28.6 %all-to-all-start.1 = ((bf16[256,8,256]{0,2,1:T(8,128)(2,1)}), bf16[256,8,256]{0,2,1:T(8,128)(2,1)S(1)}, u32[]{:S(2)}, u32[]{:S(2)}) async-start(bf16[256,8,256]{0,2,1:T(8,128)(2,1)} %bitcast.17), calls=%async_computation.1 | async-start | bytes 2097152 | tf_op jit(solution)/shard_map/all_to_all | solution.py:64
Sparse Core Ops, SparseCore 0:
  31.7 110.3 all-gather.2
  143.8 93.9 all-gather.4
where the time goes:
time: 703 us; the launch traced here: 696 us
  local copies, waits for them, and re-layouts  237 us (34%)
  other arithmetic  142 us (20%)
  waiting for transfers between devices  113 us (16%)
  matrix products  113 us (16%)
  blocking collectives  69.8 us (10%)
  between operations  13.5 us (2%)
  starting transfers between devices  7.49 us (1%)
    select_n x4, other arithmetic, one_group(): v_sel = jnp.take(v_view, listed, axis=0).reshape(shape)  100 us
    while x2, local copies, waits for them, and re-layouts, attend_all(): result = lax.map(one_group, (q_groups, block_ids))  74.3 us
    dot_general x4, matrix products, one_group(): jnp.einsum('ghqak,gakhd->gqhd', weights.astype(jnp.bfloat16), v_sel, pref...  61.9 us
    gather x4, local copies, waits for them, and re-layouts, one_group(): k_sel = jnp.take(k_view, listed, axis=0).reshape(shape)  58.9 us
    gather x4, local copies, waits for them, and re-layouts, one_group(): v_sel = jnp.take(v_view, listed, axis=0).reshape(shape)  58.9 us
    dot_general x4, matrix products, one_group(): jnp.einsum('gqhd,gakhd->ghqak', q_blk, k_sel, preferred_element_type=jnp....  51.3 us
    all_gather x1, waiting for transfers between devices, on_device(): lax.all_gather(v_loc, 'blk', axis=0, tiled=True)  49.5 us
    all_gather x1, waiting for transfers between devices, on_device(): lax.all_gather(k_loc, 'blk', axis=0, tiled=True)  43.3 us
  transfers between devices with their start and end apart: 3, of which 3 were waited for; matrix products, arithmetic and copies ran while one was open for 9% of the time, Pallas kernels for 0%

commit v1 on v0

v1 whole, which is shorter than its diff:
```python
import functools
import math

import jax
import jax.numpy as jnp
from jax import lax
from jax.experimental import pallas as pl
from jax.experimental.pallas import tpu as pltpu
from jax.sharding import Mesh, PartitionSpec as P

HD = 64
BLOCK = 128
ACT = 24
LIMIT = 2.0**100

AXES = ("near", "z", "core", "far", "y")
HEAD_AXES = ("near", "z", "y")
CHIP_AXES = ("near", "z", "far", "y")


def nt_dot(a, b):
    return lax.dot_general(a, b, (((1,), (1,)), ((), ())), preferred_element_type=jnp.float32)


def swap_halves(x):
    half = x.shape[1] // 2
    return jnp.concatenate([x[:, half:], x[:, :half]], axis=1)


def attend_kernel(place_ref, q_ref, mine_ref, other_ref, o_ref, kk, vt, acc):
    pairs = q_ref.shape[0]
    chunks = mine_ref.shape[0]
    low = lax.broadcasted_iota(jnp.int32, (BLOCK, BLOCK), 1) < HD

    for base, ref in ((0, mine_ref), (2 * chunks, other_ref)):

        @pl.loop(0, chunks)
        def _(c):
            x = ref[c, :BLOCK, :].astype(jnp.float32)
            y = swap_halves(x)
            kk[base + 2 * c] = jnp.where(low, x, y).astype(jnp.bfloat16)
            kk[base + 2 * c + 1] = jnp.where(low, y, x).astype(jnp.bfloat16)
            vt[base + 2 * c] = ref[c, BLOCK : BLOCK + HD, :]
            vt[base + 2 * c + 1] = ref[c, BLOCK + HD :, :]

    ones = jnp.ones((16, 2 * BLOCK), jnp.bfloat16)
    factor = math.log2(math.e) / math.sqrt(HD)

    @pl.loop(0, pairs)
    def _(i):
        q = q_ref[i].astype(jnp.float32) * factor
        high = q.astype(jnp.bfloat16).astype(jnp.float32)
        rest = q - high
        first = jnp.where(low, high, swap_halves(rest)).astype(jnp.bfloat16)
        second = jnp.where(low, swap_halves(high), rest).astype(jnp.bfloat16)
        zero = jnp.zeros_like(first)
        q2 = jnp.concatenate(
            [jnp.concatenate([first, zero], 1), jnp.concatenate([zero, second], 1)], 0
        )

        def scores(t):
            a = place_ref[(2 * i) * ACT + t]
            b = place_ref[(2 * i + 1) * ACT + t]
            return nt_dot(jnp.concatenate([kk[a], kk[b]], axis=1), q2)

        def whole(shift):
            total = [None, None]
            for t in range(0, ACT, 2):
                w = [jnp.exp2(scores(t + n) - shift).astype(jnp.bfloat16) for n in range(2)]
                w = jnp.concatenate(w, axis=0)
                for n in range(2):
                    g = place_ref[(2 * i + n) * ACT + t]
                    h = place_ref[(2 * i + n) * ACT + t + 1]
                    v = jnp.concatenate([vt[g], vt[h]], axis=1)
                    part = jnp.dot(
                        jnp.concatenate([v, ones], axis=0),
                        w[:, n * BLOCK : (n + 1) * BLOCK],
                        preferred_element_type=jnp.float32,
                    )
                    total[n] = part if t == 0 else total[n] + part
            acc[0], acc[1] = total

        whole(jnp.max(scores(0), axis=0, keepdims=True))
        sums = jnp.concatenate([acc[0, HD : HD + 1], acc[1, HD : HD + 1]], axis=1)
        lost = jnp.max(jnp.where(sums <= LIMIT, 0.0, 1.0))

        @pl.when(lost > 0.0)
        def _():
            top = lax.fori_loop(
                0,
                ACT,
                lambda t, m: jnp.maximum(m, jnp.max(scores(t), axis=0, keepdims=True)),
                jnp.full((1, 2 * BLOCK), -jnp.inf, jnp.float32),
            )
            whole(top)

        out = [acc[n, :HD] / acc[n, HD : HD + 1] for n in range(2)]
        o_ref[i] = jnp.transpose(jnp.concatenate(out, axis=0)).astype(jnp.bfloat16)


def attend(place, q, mine, other):
    pairs, chunks = q.shape[0], mine.shape[0]
    vmem = pl.BlockSpec(memory_space=pltpu.VMEM)
    flops = 8 * pairs * ACT * BLOCK * BLOCK * HD
    return pl.pallas_call(
        attend_kernel,
        out_shape=jax.ShapeDtypeStruct(q.shape, jnp.bfloat16),
        in_specs=[pl.BlockSpec(memory_space=pltpu.SMEM), vmem, vmem, vmem],
        out_specs=vmem,
        scratch_shapes=[
            pltpu.VMEM((4 * chunks, BLOCK, BLOCK), jnp.bfloat16),
            pltpu.VMEM((4 * chunks, HD, BLOCK), jnp.bfloat16),
            pltpu.VMEM((2, HD + 16, BLOCK), jnp.float32),
        ],
        compiler_params=pltpu.CompilerParams(vmem_limit_bytes=52 * 2**20),
        cost_estimate=pl.CostEstimate(
            flops=flops, bytes_accessed=10 * 2**20, transcendentals=2 * pairs * ACT * BLOCK * BLOCK
        ),
    )(place, q, mine, other)


def on_device(queries, keys, values, active):
    near, z, far, y = (lax.axis_size(a) for a in CHIP_AXES)
    heads = near * z * y
    blocks = queries.shape[0] // BLOCK
    core, far_id = lax.axis_index("core"), lax.axis_index("far")

    def side_by_side(x):
        x = x.reshape(blocks, BLOCK, heads, HD)
        return jnp.transpose(x, (2, 1, 0, 3)).reshape(heads, BLOCK, blocks * HD)

    q = side_by_side(queries)
    k = side_by_side(keys)
    v = jnp.transpose(values.reshape(blocks, BLOCK, heads, HD), (2, 0, 3, 1))
    v = v.reshape(heads, blocks * HD, BLOCK)
    kv = jnp.concatenate([k, v], axis=1).reshape(near, z, 1, y, 2 * BLOCK, BLOCK)
    kv = jnp.broadcast_to(kv, (near, z, far, y, 2 * BLOCK, BLOCK))
    kv = kv.reshape(near * z * far * y, 2 * BLOCK, BLOCK)

    q = lax.all_to_all(q, HEAD_AXES, 0, 0, tiled=True)
    mine = lax.all_to_all(kv, CHIP_AXES, 0, 0, tiled=True)
    other = lax.ppermute(mine, "core", [(0, 1), (1, 0)])

    per_core = far * y * blocks
    table = active.reshape(near * z, 2, far, y, blocks, ACT)
    table = lax.dynamic_slice(
        table, (0, core, far_id, 0, 0, 0), (near * z, 1, 1, y, blocks, ACT)
    ).reshape(-1)
    of_other = ((table // per_core) % 2) != core
    place = table // (2 * per_core) * per_core + table % per_core
    place = place + jnp.where(of_other, near * z * per_core, 0)

    out = attend(place, q, mine, other)
    out = lax.all_to_all(out, HEAD_AXES, 0, 0, tiled=True)
    out = out.reshape(heads, BLOCK, blocks, HD)
    return jnp.transpose(out, (2, 1, 0, 3)).reshape(queries.shape)


def solution(mesh):
    fine = Mesh(mesh.devices.reshape(2, 4, 2, 2, 4), AXES)
    tokens = P(AXES, None)
    return jax.shard_map(
        on_device,
        mesh=fine,
        in_specs=(tokens, tokens, tokens, P()),
        out_specs=tokens,
        check_vma=False,
    )
```

time: 703 us -> 247 us (0.35)
  local copies, waits for them, and re-layouts: 237 us -> 18.3 us
  other arithmetic: 142 us -> 1.65 us
  Pallas kernels: 0 us -> 118 us
  matrix products: 113 us -> 0 us
  waiting for transfers between devices: 113 us -> 16.7 us
  blocking collectives: 69.8 us -> 83.5 us
  between operations: 13.5 us -> 0.18 us
    gather x10 -> x0, local copies, waits for them, and re-layouts: 118 us -> none  [the longest x4 58.9 us: one_group(): k_sel = jnp.take(k_view, listed, axis=0).reshape(shape)]
    pallas_call x0 -> x1, Pallas kernels: none -> 118 us  [attend(): pl.pallas_call(attend_kernel, out_shape=jax.ShapeDtypeStruct(q.shape, jnp...]
    dot_general x8 -> x0, matrix products: 113 us -> none  [the longest x4 61.9 us: one_group(): jnp.einsum('ghqak,gakhd->gqhd', weights.astype(jnp.bfloat16), v_sel, pref...]
    select_n x6 -> x0, other arithmetic: 100 us -> none  [the longest x4 100 us: one_group(): v_sel = jnp.take(v_view, listed, axis=0).reshape(shape)]
    all_gather x2 -> x0, waiting for transfers between devices: 92.8 us -> none  [the longest x1 49.5 us: on_device(): lax.all_gather(v_loc, 'blk', axis=0, tiled=True)]
    while x2 -> x0, local copies, waits for them, and re-layouts: 74.3 us -> none  [attend_all(): result = lax.map(one_group, (q_groups, block_ids))]
    reduce_sum x4 -> x0, other arithmetic: 41.8 us -> none  [one_group(): total = jnp.sum(weights, axis=(3, 4))]
    unnamed x10, local copies, waits for them, and re-layouts: 34.7 us -> 4.55 us
  transfers between devices with their start and end apart: 3 -> 2, of which waited for: 3 -> 1; matrix products, arithmetic and copies ran while one was open for 9% -> 1% of each run, Pallas kernels for 0% -> 0%
where the time goes in v1:
time: 247 us
  Pallas kernels  118 us (48%)
  blocking collectives  83.5 us (34%)
  local copies, waits for them, and re-layouts  18.3 us (7%)
  waiting for transfers between devices  16.7 us (7%)
  starting transfers between devices  8.12 us (3%)
    pallas_call x1, Pallas kernels, attend(): pl.pallas_call(attend_kernel, out_shape=jax.ShapeDtypeStruct(q.shape, jnp...  118 us
    all_to_all x1, blocking collectives, on_device(): mine = lax.all_to_all(kv, CHIP_AXES, 0, 0, tiled=True)  62.5 us
    all_to_all x1, blocking collectives, on_device(): out = lax.all_to_all(out, HEAD_AXES, 0, 0, tiled=True)  21 us
    all_to_all x1, waiting for transfers between devices, on_device(): q = lax.all_to_all(q, HEAD_AXES, 0, 0, tiled=True)  16.7 us
    all_to_all x1, starting transfers between devices, on_device(): q = lax.all_to_all(q, HEAD_AXES, 0, 0, tiled=True)  8.12 us
    reshape x2, local copies, waits for them, and re-layouts, on_device(): return jnp.transpose(out, (2, 1, 0, 3)).reshape(queries.shape)  5.39 us
  transfers between devices with their start and end apart: 2, of which 1 were waited for; matrix products, arithmetic and copies ran while one was open for 1% of the time, Pallas kernels for 0%

profile of v1, /device:TPU:6, one launch (start us, length us, event | category | flops | bytes accessed | tf_op | source)
XLA Modules:
  0.0 246.7 jit_solution(2538007399520098476)
XLA Ops:
  0.0 1.5 copy.11
  1.5 0.3 reshape.38
  1.8 0.3 copy.12
  2.0 1.5 copy.13
  3.5 0.3 reshape.39
  3.8 0.3 copy.14
  4.1 0.7 copy.15
  4.8 1.6 maximum_bitcast_fusion
  6.4 3.0 %copy.16 = bf16[2,4,4,256,128]{4,3,2,1,0:T(8,128)(2,1)S(1)} copy(bf16[2,4,4,256,128]{3,4,2,1,0:T(8,128)(2,1)} %maximum_bitcast_fusion) | data formatting | bytes 4194304 | tf_op jit(solution)/shard_map/broadcast_in_dim | solution.py:137
  9.4 1.0 broadcast_in_dim.15
  10.4 0.0 copy-start
  10.4 62.5 %all_to_all.15.mine_ref = bf16[64,256,128]{2,1,0:T(8,128)(2,1)} all-to-all(bf16[64,256,128]{2,1,0:T(8,128)(2,1)S(1)} %bitcast.21), channel_id=1, replica_groups=mesh['near'=2,'z'=4,'core'=2,'far'=2,'y'=4] {'near','z','far','y'}, dimensions={0} | all-to-all | bytes 8388608 | tf_op jit(solution)/shard_map/all_to_all | solution.py:141
  72.9 0.0 collective-permute-start
  72.9 0.0 copy-done
  72.9 0.5 copy.8
  73.4 0.0 copy-start.2
  73.4 0.3 reshape.36
  73.7 0.3 copy.9
  74.0 1.3 copy.10
  75.3 8.1 %all-to-all-start = ((bf16[32,128,128]{2,1,0:T(8,128)(2,1)}), bf16[32,128,128]{2,1,0:T(8,128)(2,1)S(1)}, u32[]{:S(2)}, u32[]{:S(2)}) async-start(bf16[32,128,128]{2,1,0:T(8,128)(2,1)} %copy.10), calls=%async_computation | async-start | bytes 2097152 | tf_op jit(solution)/shard_map/all_to_all | solution.py:140
  83.5 0.0 copy-done.2
  83.5 0.1 copy.7
  83.6 0.1 reshape.35
  83.7 16.7 %all-to-all-done.q_ref = bf16[32,128,128]{2,1,0:T(8,128)(2,1)S(1)} async-done(((bf16[32,128,128]{2,1,0:T(8,128)(2,1)}), bf16[32,128,128]{2,1,0:T(8,128)(2,1)S(1)}, u32[]{:S(2)}, u32[]{:S(2)}) %all-to-all-start) | async-done | bytes 1048608 | tf_op jit(solution)/shard_map/all_to_all | solution.py:140
  100.4 0.0 copy-start.1
  100.4 0.0 collective-permute-done.other_ref
  100.4 1.0 copy-done.1
  101.4 118.3 %shard_map.46 = bf16[32,128,128]{2,1,0:T(8,128)(2,1)S(1)} custom-call(s32[1536]{0:T(1024)S(1)} %fusion.3.place_ref, bf16[32,128,128]{2,1,0:T(8,128)(2,1)} %copy-done.1, bf16[64,256,128]{2,1,0:T(8,128)(2,1)} %all_to_all.15.mine_ref, bf16[64,256,128]{2,1,0:T(8,128)(2,1)} %collective-permute-done.other_ref), custom_call_target="tpu_custom_call" | custom-call | flops 6442450944 | bytes 10485760 | tf_op jit(solution)/shard_map/pallas_call | solution.py:105
  219.7 21.0 %all_to_all.16 = bf16[32,128,128]{2,1,0:T(8,128)(2,1)S(1)} all-to-all(bf16[32,128,128]{2,1,0:T(8,128)(2,1)S(1)} %shard_map.46), channel_id=1, replica_groups=mesh['near'=2,'z'=4,'core'=2,'far'=2,'y'=4] {'near','z','y'}, dimensions={0} | all-to-all | bytes 2097152 | tf_op jit(solution)/shard_map/all_to_all | solution.py:154
  240.7 0.7 copy.17
  241.3 3.0 %copy.20 = bf16[2,128,32,64]{3,2,1,0:T(8,128)(2,1)S(1)} copy(bf16[2,128,32,64]{1,3,0,2:T(8,128)(2,1)S(1)} %bitcast.22) | data formatting | bytes 2097152 | tf_op jit(solution)/shard_map/reshape | solution.py:156
  244.3 2.4 reshape.43
  (2 shorter events, 0.0 us)
Async XLA Ops:
  10.4 62.5 %copy-start = (bf16[256,2048]{1,0:T(8,128)(2,1)S(1)}, bf16[256,2048]{1,0:T(8,128)(2,1)}, u32[]{:S(2)}) copy-start(bf16[256,2048]{1,0:T(8,128)(2,1)} %param.4) | copy-start | bytes 3145732
  72.9 27.5 %collective-permute-start = (bf16[64,256,128]{2,1,0:T(8,128)(2,1)}, bf16[64,256,128]{2,1,0:T(8,128)(2,1)}, u32[]{:S(2)}, u32[]{:S(2)}) collective-permute-start(bf16[64,256,128]{2,1,0:T(8,128)(2,1)} %all_to_all.15.mine_ref), channel_id=1, source_target_pairs={{0,8},{8,0},{1,9},{9,1},{2,10},{10,2},{3,11},{11,3},{4,12},{12,4},... | collective-permute-start | bytes 12582920 | tf_op jit(solution)/shard_map/ppermute | solution.py:142
  73.4 10.0 %copy-start.2 = (s32[256,24]{0,1:T(8,128)S(1)}, s32[256,24]{0,1:T(8,128)}, u32[]{:S(2)}) copy-start(s32[256,24]{0,1:T(8,128)} %param.7) | copy-start | bytes 73732
  75.3 25.1 %all-to-all-start = ((bf16[32,128,128]{2,1,0:T(8,128)(2,1)}), bf16[32,128,128]{2,1,0:T(8,128)(2,1)S(1)}, u32[]{:S(2)}, u32[]{:S(2)}) async-start(bf16[32,128,128]{2,1,0:T(8,128)(2,1)} %copy.10), calls=%async_computation | async-start | bytes 2097152 | tf_op jit(solution)/shard_map/all_to_all | solution.py:140
  100.4 1.0 copy-start.1

commit v2 on v1

v2 whole, which is shorter than its diff:
```python
import functools
import math

import jax
import jax.numpy as jnp
from jax import lax
from jax.experimental import pallas as pl
from jax.experimental.pallas import tpu as pltpu
from jax.sharding import Mesh, PartitionSpec as P

HD = 64
BLOCK = 128
ACT = 24
LIMIT = 2.0**100

AXES = ("near", "z", "core", "far", "y")
HEAD_AXES = ("near", "z", "y")
CHIP_AXES = ("near", "z", "far", "y")


def swap_halves(x):
    half = x.shape[1] // 2
    return jnp.concatenate([x[:, half:], x[:, :half]], axis=1)


def attend_kernel(
    place_ref, q_ref, mine_ref, other_ref, o_ref, kp, kk, vt, q2, shift, sums, sems
):
    pairs = q_ref.shape[0]
    chunks = mine_ref.shape[0]
    low = lax.broadcasted_iota(jnp.int32, (BLOCK, BLOCK), 1) < HD

    copies = []
    for n, ref in enumerate((mine_ref, other_ref)):
        there = pl.ds(n * chunks, chunks)
        copies.append(pltpu.make_async_copy(ref.at[:, :BLOCK, :], kp.at[there], sems.at[n]))
        copies.append(pltpu.make_async_copy(ref.at[:, BLOCK:, :], vt.at[there], sems.at[2 + n]))
    for copy in copies:
        copy.start()

    for n in range(2):
        copies[2 * n].wait()

        @pl.loop(n * chunks, (n + 1) * chunks, step=8)
        def _(first):
            for c in [first + u for u in range(8)]:
                x = kp[c]
                y = swap_halves(x)
                kk[2 * c] = jnp.where(low, x, y)
                kk[2 * c + 1] = jnp.where(low, y, x)

    def scores(i, t, n):
        rows = []
        for j in range(t, t + n):
            a = place_ref[2 * i * ACT + j]
            b = place_ref[(2 * i + 1) * ACT + j]
            rows.append(jnp.concatenate([kk[a], kk[b]], axis=1))
        return jnp.dot(
            jnp.concatenate(rows, axis=0), q2[i], preferred_element_type=jnp.float32
        )

    def scores_at(i, t):
        a = place_ref[2 * i * ACT + t]
        b = place_ref[(2 * i + 1) * ACT + t]
        x = jnp.concatenate([kk[a], kk[b]], axis=1)
        return jnp.dot(x, q2[i], preferred_element_type=jnp.float32)

    factor = math.log2(math.e) / math.sqrt(HD)

    @pl.loop(0, pairs, step=4)
    def _(first):
        for i in [first + u for u in range(4)]:
            q = q_ref[i].astype(jnp.float32) * factor
            high = q.astype(jnp.bfloat16).astype(jnp.float32)
            rest = q - high
            a = jnp.transpose(jnp.where(low, high, swap_halves(rest)))
            b = jnp.transpose(jnp.where(low, swap_halves(high), rest))
            zero = jnp.zeros((BLOCK, BLOCK), jnp.bfloat16)
            q2[i, :BLOCK, :BLOCK] = a.astype(jnp.bfloat16)
            q2[i, :BLOCK, BLOCK:] = zero
            q2[i, BLOCK:, :BLOCK] = zero
            q2[i, BLOCK:, BLOCK:] = b.astype(jnp.bfloat16)
        for i in [first + u for u in range(4)]:
            shift[i] = jnp.max(scores(i, 0, 1), axis=0, keepdims=True)

    for n in range(2):
        copies[2 * n + 1].wait()

    def values(i, n, t, count):
        blocks = []
        for j in range(t, t + count):
            g = place_ref[(2 * i + n) * ACT + j]
            blocks.append(vt[g // 2, pl.ds(pl.multiple_of((g % 2) * HD, HD), HD), :])
        return jnp.concatenate(blocks, axis=1)

    def whole(i, count):
        ones = jnp.ones((16, count * BLOCK), jnp.bfloat16)
        total = None
        for t in range(0, ACT, count):
            w = jnp.exp2(scores(i, t, count) - shift[i]).astype(jnp.bfloat16)
            v = jnp.concatenate([values(i, 0, t, count), values(i, 1, t, count), ones], axis=0)
            part = jnp.dot(v, w, preferred_element_type=jnp.float32)
            total = part if total is None else total + part
        sums[i] = total[2 * HD : 2 * HD + 1]
        inverse = 1.0 / sums[i]
        out = jnp.concatenate(
            [
                total[:HD, :BLOCK] * inverse[:, :BLOCK],
                total[HD : 2 * HD, BLOCK:] * inverse[:, BLOCK:],
            ],
            axis=0,
        )
        o_ref[i] = jnp.transpose(out).astype(jnp.bfloat16)

    @pl.loop(0, pairs, step=4)
    def _(first):
        for u in range(4):
            whole(first + u, 8)

    def lost(s):
        return jnp.max(jnp.where(s <= LIMIT, 0.0, 1.0)) > 0.0

    @pl.when(lost(sums[...]))
    def _():
        @pl.loop(0, pairs)
        def _(i):
            @pl.when(lost(sums[i]))
            def _():
                shift[i] = lax.fori_loop(
                    0,
                    ACT,
                    lambda t, top: jnp.maximum(
                        top, jnp.max(scores_at(i, t), axis=0, keepdims=True)
                    ),
                    jnp.full((1, 2 * BLOCK), -jnp.inf, jnp.float32),
                )
                whole(i, 2)


def attend(place, q, mine, other):
    pairs, chunks = q.shape[0], mine.shape[0]
    vmem = pl.BlockSpec(memory_space=pltpu.VMEM)
    anywhere = pl.BlockSpec(memory_space=pl.ANY)
    return pl.pallas_call(
        attend_kernel,
        out_shape=jax.ShapeDtypeStruct(q.shape, jnp.bfloat16),
        in_specs=[pl.BlockSpec(memory_space=pltpu.SMEM), vmem, anywhere, anywhere],
        out_specs=vmem,
        scratch_shapes=[
            pltpu.VMEM((2 * chunks, BLOCK, BLOCK), jnp.bfloat16),
            pltpu.VMEM((4 * chunks, BLOCK, BLOCK), jnp.bfloat16),
            pltpu.VMEM((2 * chunks, BLOCK, BLOCK), jnp.bfloat16),
            pltpu.VMEM((pairs, 2 * BLOCK, 2 * BLOCK), jnp.bfloat16),
            pltpu.VMEM((pairs, 1, 2 * BLOCK), jnp.float32),
            pltpu.VMEM((pairs, 1, 2 * BLOCK), jnp.float32),
            pltpu.SemaphoreType.DMA((4,)),
        ],
        compiler_params=pltpu.CompilerParams(vmem_limit_bytes=48 * 2**20),
        cost_estimate=pl.CostEstimate(
            flops=8 * pairs * ACT * BLOCK * BLOCK * HD,
            bytes_accessed=10 * 2**20,
            transcendentals=2 * pairs * ACT * BLOCK * BLOCK,
        ),
    )(place, q, mine, other)


def on_device(queries, keys, values, active):
    near, z, far, y = (lax.axis_size(a) for a in CHIP_AXES)
    heads = near * z * y
    blocks = queries.shape[0] // BLOCK
    core, far_id = lax.axis_index("core"), lax.axis_index("far")

    def side_by_side(x):
        x = x.reshape(blocks, BLOCK, heads, HD)
        return jnp.transpose(x, (2, 1, 0, 3)).reshape(heads, BLOCK, blocks * HD)

    q = side_by_side(queries)
    k = side_by_side(keys)
    v = jnp.transpose(values.reshape(blocks, BLOCK, heads, HD), (2, 0, 3, 1))
    v = v.reshape(heads, blocks * HD, BLOCK)
    kv = jnp.concatenate([k, v], axis=1).reshape(near, z, 1, y, 2 * BLOCK, BLOCK)
    kv = jnp.broadcast_to(kv, (near, z, far, y, 2 * BLOCK, BLOCK))
    kv = kv.reshape(near * z * far * y, 2 * BLOCK, BLOCK)

    q = lax.all_to_all(q, HEAD_AXES, 0, 0, tiled=True)
    mine = lax.all_to_all(kv, CHIP_AXES, 0, 0, tiled=True)
    other = lax.ppermute(mine, "core", [(0, 1), (1, 0)])

    per_core = far * y * blocks
    table = active.reshape(near * z, 2, far, y, blocks, ACT)
    table = lax.dynamic_slice(
        table, (0, core, far_id, 0, 0, 0), (near * z, 1, 1, y, blocks, ACT)
    ).reshape(-1)
    of_other = ((table // per_core) % 2) != core
    place = table // (2 * per_core) * per_core + table % per_core
    place = place + jnp.where(of_other, near * z * per_core, 0)

    out = attend(place, q, mine, other)
    out = lax.all_to_all(out, HEAD_AXES, 0, 0, tiled=True)
    out = out.reshape(heads, BLOCK, blocks, HD)
    return jnp.transpose(out, (2, 1, 0, 3)).reshape(queries.shape)


def solution(mesh):
    fine = Mesh(mesh.devices.reshape(2, 4, 2, 2, 4), AXES)
    tokens = P(AXES, None)
    return jax.shard_map(
        on_device,
        mesh=fine,
        in_specs=(tokens, tokens, tokens, P()),
        out_specs=tokens,
        check_vma=False,
    )
```

time: 247 us -> 163 us (0.66)
  Pallas kernels: 118 us -> 35.1 us
    pallas_call x1, Pallas kernels: 118 us -> 35.1 us  [attend(): pl.pallas_call(attend_kernel, out_shape=jax.ShapeDtypeStruct(q.shape, jnp...]
  transfers between devices with their start and end apart: 2 -> 2, of which waited for: 1 -> 1; matrix products, arithmetic and copies ran while one was open for 1% -> 2% of each run, Pallas kernels for 0% -> 0%
where the time goes in v2:
time: 163 us; the launch traced here: 162 us
  blocking collectives  83.5 us (51%)
  Pallas kernels  35.1 us (22%)
  local copies, waits for them, and re-layouts  17.3 us (11%)
  waiting for transfers between devices  16.7 us (10%)
  starting transfers between devices  8.12 us (5%)
    all_to_all x1, blocking collectives, on_device(): mine = lax.all_to_all(kv, CHIP_AXES, 0, 0, tiled=True)  62.5 us
    pallas_call x1, Pallas kernels, attend(): pl.pallas_call(attend_kernel, out_shape=jax.ShapeDtypeStruct(q.shape, jnp...  35.1 us
    all_to_all x1, blocking collectives, on_device(): out = lax.all_to_all(out, HEAD_AXES, 0, 0, tiled=True)  21 us
    all_to_all x1, waiting for transfers between devices, on_device(): q = lax.all_to_all(q, HEAD_AXES, 0, 0, tiled=True)  16.7 us
    all_to_all x1, starting transfers between devices, on_device(): q = lax.all_to_all(q, HEAD_AXES, 0, 0, tiled=True)  8.12 us
    reshape x2, local copies, waits for them, and re-layouts, on_device(): return jnp.transpose(out, (2, 1, 0, 3)).reshape(queries.shape)  5.39 us
    broadcast_in_dim x2, local copies, waits for them, and re-layouts, on_device(): kv = jnp.broadcast_to(kv, (near, z, far, y, 2 * BLOCK, BLOCK))  3.97 us
    unnamed x8, local copies, waits for them, and re-layouts  3.58 us
  transfers between devices with their start and end apart: 2, of which 1 were waited for; matrix products, arithmetic and copies ran while one was open for 2% of the time, Pallas kernels for 0%

profile of v2, /device:TPU:6, one launch (start us, length us, event | category | flops | bytes accessed | tf_op | source)
XLA Modules:
  0.0 162.5 jit_solution(17690789323051867374)
XLA Ops:
  0.0 1.5 copy.11
  1.5 0.3 reshape.38
  1.8 0.3 copy.12
  2.0 1.5 copy.13
  3.5 0.3 reshape.39
  3.8 0.3 copy.14
  4.1 0.7 copy.15
  4.8 1.6 maximum_bitcast_fusion
  6.4 3.0 %copy.16 = bf16[2,4,4,256,128]{4,3,2,1,0:T(8,128)(2,1)S(1)} copy(bf16[2,4,4,256,128]{3,4,2,1,0:T(8,128)(2,1)} %maximum_bitcast_fusion) | data formatting | bytes 4194304 | tf_op jit(solution)/shard_map/broadcast_in_dim | solution.py:182
  9.3 1.0 broadcast_in_dim.15
  10.3 0.0 copy-start
  10.4 62.5 %all_to_all.15.mine_ref = bf16[64,256,128]{2,1,0:T(8,128)(2,1)} all-to-all(bf16[64,256,128]{2,1,0:T(8,128)(2,1)S(1)} %bitcast.21), channel_id=1, replica_groups=mesh['near'=2,'z'=4,'core'=2,'far'=2,'y'=4] {'near','z','far','y'}, dimensions={0} | all-to-all | bytes 8388608 | tf_op jit(solution)/shard_map/all_to_all | solution.py:186
  72.9 0.0 collective-permute-start
  72.9 0.0 copy-done
  72.9 0.5 copy.8
  73.4 0.0 copy-start.1
  73.4 0.3 reshape.36
  73.7 0.3 copy.9
  74.0 1.3 copy.10
  75.3 8.1 %all-to-all-start = ((bf16[32,128,128]{2,1,0:T(8,128)(2,1)}), bf16[32,128,128]{2,1,0:T(8,128)(2,1)S(1)}, u32[]{:S(2)}, u32[]{:S(2)}) async-start(bf16[32,128,128]{2,1,0:T(8,128)(2,1)} %copy.10), calls=%async_computation | async-start | bytes 2097152 | tf_op jit(solution)/shard_map/all_to_all | solution.py:185
  83.4 0.0 copy-done.1
  83.4 0.1 copy.7
  83.5 0.1 reshape.35
  83.7 16.7 %all-to-all-done.q_ref = bf16[32,128,128]{2,1,0:T(8,128)(2,1)S(1)} async-done(((bf16[32,128,128]{2,1,0:T(8,128)(2,1)}), bf16[32,128,128]{2,1,0:T(8,128)(2,1)S(1)}, u32[]{:S(2)}, u32[]{:S(2)}) %all-to-all-start) | async-done | bytes 1048608 | tf_op jit(solution)/shard_map/all_to_all | solution.py:185
  100.4 0.0 collective-permute-done.other_ref
  100.4 35.1 %shard_map.46 = bf16[32,128,128]{2,1,0:T(8,128)(2,1)S(1)} custom-call(s32[1536]{0:T(1024)S(1)} %fusion.3.place_ref, bf16[32,128,128]{2,1,0:T(8,128)(2,1)S(1)} %all-to-all-done.q_ref, bf16[64,256,128]{2,1,0:T(8,128)(2,1)} %all_to_all.15.mine_ref, bf16[64,256,128]{2,1,0:T(8,128)(2,1)} %collective-permute-done.other_ref), custom_call_target="tpu_custom_call" | custom-call | flops 6442450944 | bytes 10485760 | tf_op jit(solution)/shard_map/pallas_call | solution.py:144
  135.5 21.0 %all_to_all.16 = bf16[32,128,128]{2,1,0:T(8,128)(2,1)S(1)} all-to-all(bf16[32,128,128]{2,1,0:T(8,128)(2,1)S(1)} %shard_map.46), channel_id=1, replica_groups=mesh['near'=2,'z'=4,'core'=2,'far'=2,'y'=4] {'near','z','y'}, dimensions={0} | all-to-all | bytes 2097152 | tf_op jit(solution)/shard_map/all_to_all | solution.py:199
  156.4 0.7 copy.17
  157.1 3.0 %copy.20 = bf16[2,128,32,64]{3,2,1,0:T(8,128)(2,1)S(1)} copy(bf16[2,128,32,64]{1,3,0,2:T(8,128)(2,1)S(1)} %bitcast.22) | data formatting | bytes 2097152 | tf_op jit(solution)/shard_map/reshape | solution.py:201
  160.1 2.4 %reshape.43 = bf16[256,2048]{1,0:T(8,128)(2,1)} reshape(bf16[2,128,32,64]{3,2,1,0:T(8,128)(2,1)S(1)} %copy.20) | data formatting | bytes 2097152 | tf_op jit(solution)/shard_map/reshape | solution.py:201
  (2 shorter events, 0.0 us)
Async XLA Ops:
  10.3 62.5 %copy-start = (bf16[256,2048]{1,0:T(8,128)(2,1)S(1)}, bf16[256,2048]{1,0:T(8,128)(2,1)}, u32[]{:S(2)}) copy-start(bf16[256,2048]{1,0:T(8,128)(2,1)} %param.4) | copy-start | bytes 3145732
  72.9 27.5 %collective-permute-start = (bf16[64,256,128]{2,1,0:T(8,128)(2,1)}, bf16[64,256,128]{2,1,0:T(8,128)(2,1)}, u32[]{:S(2)}, u32[]{:S(2)}) collective-permute-start(bf16[64,256,128]{2,1,0:T(8,128)(2,1)} %all_to_all.15.mine_ref), channel_id=1, source_target_pairs={{0,8},{8,0},{1,9},{9,1},{2,10},{10,2},{3,11},{11,3},{4,12},{12,4},... | collective-permute-start | bytes 12582920 | tf_op jit(solution)/shard_map/ppermute | solution.py:187
  73.4 10.0 %copy-start.1 = (s32[256,24]{0,1:T(8,128)S(1)}, s32[256,24]{0,1:T(8,128)}, u32[]{:S(2)}) copy-start(s32[256,24]{0,1:T(8,128)} %param.7) | copy-start | bytes 73732
  75.3 25.1 %all-to-all-start = ((bf16[32,128,128]{2,1,0:T(8,128)(2,1)}), bf16[32,128,128]{2,1,0:T(8,128)(2,1)S(1)}, u32[]{:S(2)}, u32[]{:S(2)}) async-start(bf16[32,128,128]{2,1,0:T(8,128)(2,1)} %copy.10), calls=%async_computation | async-start | bytes 2097152 | tf_op jit(solution)/shard_map/all_to_all | solution.py:185

commit v3 on v2

v3 whole, which is shorter than its diff:
```python
import functools
import math

import jax
import jax.numpy as jnp
from jax import lax
from jax.experimental import pallas as pl
from jax.experimental.pallas import tpu as pltpu
from jax.sharding import Mesh, PartitionSpec as P

HD = 64
BLOCK = 128
ACT = 24
LIMIT = 2.0**100

AXES = ("near", "z", "core", "far", "y")
HEAD_AXES = ("near", "z", "y")
CHIP_AXES = ("near", "z", "far", "y")


def swap_halves(x):
    half = x.shape[1] // 2
    return jnp.concatenate([x[:, half:], x[:, :half]], axis=1)


def both_blocks(x):
    low = lax.broadcasted_iota(jnp.int32, (BLOCK, 2 * HD), 1) < HD
    top, bottom = x[:BLOCK], x[BLOCK:]
    return jnp.where(low, top, swap_halves(bottom)), jnp.where(low, swap_halves(top), bottom)


def pack_kernel(q_ref, k_ref, v_ref, q_out, kv_out):
    for pair in range(q_out.shape[0] // 2):
        columns = pl.ds(pair * 2 * HD, 2 * HD)
        for n, block in enumerate(both_blocks(q_ref[:, columns])):
            q_out[2 * pair + n] = block
        keys = both_blocks(k_ref[:, columns])
        v = jnp.transpose(v_ref[:, columns])
        for n in range(2):
            rows = v[n * HD : (n + 1) * HD]
            for copy in range(kv_out.shape[1]):
                kv_out[0, copy, 2 * pair + n, :BLOCK] = keys[n]
                kv_out[0, copy, 2 * pair + n, BLOCK : BLOCK + HD] = rows[:, :BLOCK]
                kv_out[0, copy, 2 * pair + n, BLOCK + HD :] = rows[:, BLOCK:]


def pack(queries, keys, values, groups, copies, heads):
    rows, width = queries.shape
    block = pl.BlockSpec((rows, width // groups), lambda g: (0, g))
    return pl.pallas_call(
        pack_kernel,
        grid=(groups,),
        out_shape=(
            jax.ShapeDtypeStruct((groups * heads, BLOCK, 2 * HD), queries.dtype),
            jax.ShapeDtypeStruct((groups, copies, heads, 2 * BLOCK, BLOCK), keys.dtype),
        ),
        in_specs=[block] * 3,
        out_specs=(
            pl.BlockSpec((heads, BLOCK, 2 * HD), lambda g: (g, 0, 0)),
            pl.BlockSpec((1, copies, heads, 2 * BLOCK, BLOCK), lambda g: (g, 0, 0, 0, 0)),
        ),
    )(queries, keys, values)


def unpack_kernel(x_ref, o_ref):
    low = lax.broadcasted_iota(jnp.int32, (BLOCK, 2 * HD), 1) < HD
    for pair in range(x_ref.shape[0] // 2):
        columns = pl.ds(pair * 2 * HD, 2 * HD)
        x, y = x_ref[2 * pair], x_ref[2 * pair + 1]
        o_ref[:BLOCK, columns] = jnp.where(low, x, swap_halves(y))
        o_ref[BLOCK:, columns] = jnp.where(low, swap_halves(x), y)


def unpack(x, groups):
    heads = x.shape[0]
    return pl.pallas_call(
        unpack_kernel,
        grid=(groups,),
        out_shape=jax.ShapeDtypeStruct((2 * BLOCK, heads * HD), x.dtype),
        in_specs=[pl.BlockSpec((heads // groups, BLOCK, 2 * HD), lambda g: (g, 0, 0))],
        out_specs=pl.BlockSpec((2 * BLOCK, heads * HD // groups), lambda g: (0, g)),
    )(x)


def attend_kernel(
    place_ref, q_ref, mine_ref, other_ref, o_ref, kk, vt, q2, shift, sums, sems
):
    pairs = q_ref.shape[0]
    chunks = mine_ref.shape[0]
    low = lax.broadcasted_iota(jnp.int32, (BLOCK, BLOCK), 1) < HD

    keys, rest = [], []
    for n, ref in enumerate((mine_ref, other_ref)):
        first, second = pl.ds(n * chunks, chunks), pl.ds((2 + n) * chunks, chunks)
        sem = sems.at[n]
        keys.append(pltpu.make_async_copy(ref.at[:, :BLOCK, :], kk.at[first], sem.at[0]))
        upper, lower = ref.at[:, BLOCK : BLOCK + HD, :], ref.at[:, BLOCK + HD :, :]
        rest.append(pltpu.make_async_copy(upper, vt.at[first], sem.at[1]))
        rest.append(pltpu.make_async_copy(lower, vt.at[second], sem.at[2]))
    for copy in keys + rest:
        copy.start()

    for n in range(2):
        keys[n].wait()

        @pl.loop(n * chunks, (n + 1) * chunks, step=8)
        def _(first):
            for c in [first + u for u in range(8)]:
                kk[2 * chunks + c] = swap_halves(kk[c])

    def scores(i, t, n):
        rows = []
        for j in range(n):
            a = place_ref[2 * i * ACT + t + j]
            b = place_ref[(2 * (pairs + i) + 1) * ACT + t + j]
            rows.append(jnp.where(low, kk[a], kk[b]))
        rows = jnp.concatenate(rows, axis=0) if n > 1 else rows[0]
        return jnp.dot(rows, q2[i], preferred_element_type=jnp.float32)

    factor = math.log2(math.e) / math.sqrt(HD)

    @pl.loop(0, pairs, step=4)
    def _(first):
        for i in [first + u for u in range(4)]:
            q = jnp.transpose(q_ref[i].astype(jnp.float32)).astype(jnp.bfloat16)
            zero = jnp.zeros((HD, BLOCK), jnp.bfloat16)
            q2[i, :HD, :BLOCK] = q[:HD]
            q2[i, :HD, BLOCK:] = zero
            q2[i, HD:, :BLOCK] = zero
            q2[i, HD:, BLOCK:] = q[HD:]
        for i in [first + u for u in range(4)]:
            shift[i] = factor * jnp.max(scores(i, 0, 1), axis=0, keepdims=True)

    for copy in rest:
        copy.wait()

    def values(i, n, t, count):
        blocks = [vt[place_ref[(2 * i + n) * ACT + t + j]] for j in range(count)]
        return jnp.concatenate(blocks, axis=1)

    def weights(i, s):
        return jnp.exp2(s * factor - shift[i]).astype(jnp.bfloat16)

    def weighted(i, t, w, count):
        ones = jnp.ones((16, count * BLOCK), jnp.bfloat16)
        v = jnp.concatenate([values(i, 0, t, count), values(i, 1, t, count), ones], axis=0)
        return jnp.dot(v, w, preferred_element_type=jnp.float32)

    def finish(i, total):
        sums[i] = total[2 * HD : 2 * HD + 1]
        inverse = 1.0 / sums[i]
        out = jnp.concatenate(
            [
                total[:HD, :BLOCK] * inverse[:, :BLOCK],
                total[HD : 2 * HD, BLOCK:] * inverse[:, BLOCK:],
            ],
            axis=0,
        )
        o_ref[i] = jnp.transpose(out).astype(jnp.bfloat16)

    def run(todo, count):
        steps = [(i, t) for i in todo for t in range(0, ACT, count)]
        score, weight, total = {}, {}, None
        for k in range(len(steps) + 2):
            if k < len(steps):
                score[k] = scores(*steps[k], count)
            if 0 < k <= len(steps):
                weight[k - 1] = weights(steps[k - 1][0], score.pop(k - 1))
            if 1 < k:
                i, t = steps[k - 2]
                part = weighted(i, t, weight.pop(k - 2), count)
                total = part if t == 0 else total + part
                if t + count == ACT:
                    finish(i, total)

    @pl.loop(0, pairs, step=4)
    def _(first):
        run([first + u for u in range(4)], 4)

    def lost(s):
        return jnp.max(jnp.where(s <= LIMIT, 0.0, 1.0)) > 0.0

    @pl.when(lost(sums[...]))
    def _():
        @pl.loop(0, pairs)
        def _(i):
            @pl.when(lost(sums[i]))
            def _():
                def higher(t, top):
                    return jnp.maximum(top, jnp.max(scores(i, t, 1), axis=0, keepdims=True))

                lowest = jnp.full((1, 2 * BLOCK), -jnp.inf, jnp.float32)
                shift[i] = factor * lax.fori_loop(0, ACT, higher, lowest)
                run([i], 2)


def attend(place, q, mine, other):
    pairs, chunks = q.shape[0], mine.shape[0]
    vmem = pl.BlockSpec(memory_space=pltpu.VMEM)
    anywhere = pl.BlockSpec(memory_space=pl.ANY)
    return pl.pallas_call(
        attend_kernel,
        out_shape=jax.ShapeDtypeStruct(q.shape, jnp.bfloat16),
        in_specs=[pl.BlockSpec(memory_space=pltpu.SMEM), vmem, anywhere, anywhere],
        out_specs=vmem,
        scratch_shapes=[
            pltpu.VMEM((4 * chunks, BLOCK, BLOCK), jnp.bfloat16),
            pltpu.VMEM((4 * chunks, HD, BLOCK), jnp.bfloat16),
            pltpu.VMEM((pairs, BLOCK, 2 * BLOCK), jnp.bfloat16),
            pltpu.VMEM((pairs, 1, 2 * BLOCK), jnp.float32),
            pltpu.VMEM((pairs, 1, 2 * BLOCK), jnp.float32),
            pltpu.SemaphoreType.DMA((2, 3)),
        ],
        compiler_params=pltpu.CompilerParams(vmem_limit_bytes=48 * 2**20),
        cost_estimate=pl.CostEstimate(
            flops=8 * pairs * ACT * BLOCK * BLOCK * HD,
            bytes_accessed=10 * 2**20,
            transcendentals=2 * pairs * ACT * BLOCK * BLOCK,
        ),
    )(place, q, mine, other)


def on_device(queries, keys, values, active):
    near, z, far, y = (lax.axis_size(a) for a in CHIP_AXES)
    heads = near * z * y
    blocks = queries.shape[0] // BLOCK
    core, far_id = lax.axis_index("core"), lax.axis_index("far")

    q, kv = pack(queries, keys, values, near * z, far, y)
    kv = kv.reshape(near * z * far * y, 2 * BLOCK, BLOCK)

    q = lax.all_to_all(q, HEAD_AXES, 0, 0, tiled=True)
    mine = lax.all_to_all(kv, CHIP_AXES, 0, 0, tiled=True)
    other = lax.ppermute(mine, "core", [(0, 1), (1, 0)])

    per_core = far * y * blocks
    chunks = near * z * far * y
    table = active.reshape(near * z, 2, far, y, blocks, ACT)
    table = lax.dynamic_slice(
        table, (0, core, far_id, 0, 0, 0), (near * z, 1, 1, y, blocks, ACT)
    ).reshape(-1)
    of_other = ((table // per_core) % 2) != core
    chunk = (table // (2 * per_core) * per_core + table % per_core) // 2
    chunk = chunk + jnp.where(of_other, chunks, 0)
    place = jnp.concatenate(
        [chunk + 2 * chunks * (table % 2), chunk + 2 * chunks * (1 - table % 2)]
    )

    out = attend(place, q, mine, other)
    out = lax.all_to_all(out, HEAD_AXES, 0, 0, tiled=True)
    return unpack(out, near * z)


def solution(mesh):
    fine = Mesh(mesh.devices.reshape(2, 4, 2, 2, 4), AXES)
    tokens = P(AXES, None)
    return jax.shard_map(
        on_device,
        mesh=fine,
        in_specs=(tokens, tokens, tokens, P()),
        out_specs=tokens,
        check_vma=False,
    )
```

time: 163 us -> 154 us (0.945)
  local copies, waits for them, and re-layouts: 17.3 us -> 0.21 us
  Pallas kernels: 35.1 us -> 44.6 us
    pallas_call x0 -> x2, Pallas kernels: none -> 12.7 us  [the longest x1 7.18 us: pack(): pl.pallas_call(pack_kernel, grid=(groups,), out_shape=(jax.ShapeDtypeStru...]
    reshape x6 -> x0, local copies, waits for them, and re-layouts: 7.56 us -> none  [the longest x2 5.39 us: on_device(): return jnp.transpose(out, (2, 1, 0, 3)).reshape(queries.shape)]
    broadcast_in_dim x2 -> x0, local copies, waits for them, and re-layouts: 3.97 us -> none  [on_device(): kv = jnp.broadcast_to(kv, (near, z, far, y, 2 * BLOCK, BLOCK))]
    unnamed x8 -> x3, local copies, waits for them, and re-layouts: 3.58 us -> 0.1 us
    pallas_call x1, Pallas kernels: 35.1 us -> 31.9 us  [attend(): pl.pallas_call(attend_kernel, out_shape=jax.ShapeDtypeStruct(q.shape, jnp...]
  transfers between devices with their start and end apart: 2 -> 2, of which waited for: 1 -> 1; matrix products, arithmetic and copies ran while one was open for 2% -> 0% of each run, Pallas kernels for 0% -> 0%
where the time goes in v3:
time: 154 us; the launch traced here: 153 us
  blocking collectives  83.7 us (54%)
  Pallas kernels  44.6 us (29%)
  waiting for transfers between devices  16.7 us (11%)
  starting transfers between devices  8.12 us (5%)
    all_to_all x1, blocking collectives, on_device(): mine = lax.all_to_all(kv, CHIP_AXES, 0, 0, tiled=True)  62.7 us
    pallas_call x1, Pallas kernels, attend(): pl.pallas_call(attend_kernel, out_shape=jax.ShapeDtypeStruct(q.shape, jnp...  31.9 us
    all_to_all x1, blocking collectives, on_device(): out = lax.all_to_all(out, HEAD_AXES, 0, 0, tiled=True)  21.1 us
    all_to_all x1, waiting for transfers between devices, on_device(): q = lax.all_to_all(q, HEAD_AXES, 0, 0, tiled=True)  16.7 us
    all_to_all x1, starting transfers between devices, on_device(): q = lax.all_to_all(q, HEAD_AXES, 0, 0, tiled=True)  8.12 us
    pallas_call x1, Pallas kernels, pack(): pl.pallas_call(pack_kernel, grid=(groups,), out_shape=(jax.ShapeDtypeStru...  7.18 us
    pallas_call x1, Pallas kernels, unpack(): pl.pallas_call(unpack_kernel, grid=(groups,), out_shape=jax.ShapeDtypeStr...  5.51 us
  transfers between devices with their start and end apart: 2, of which 1 were waited for; matrix products, arithmetic and copies ran while one was open for 0% of the time, Pallas kernels for 0%

profile of v3, /device:TPU:6, one launch (start us, length us, event | category | flops | bytes accessed | tf_op | source)
XLA Modules:
  0.0 153.4 jit_solution(17730069071163986271)
XLA Ops:
  0.0 7.2 %shard_map.46 = (bf16[32,128,128]{2,1,0:T(8,128)(2,1)}, bf16[8,2,4,256,128]{4,3,2,1,0:T(8,128)(2,1)}) custom-call(bf16[256,2048]{1,0:T(8,128)(2,1)} %q_ref.1, bf16[256,2048]{1,0:T(8,128)(2,1)} %k_ref.1, bf16[256,2048]{1,0:T(8,128)(2,1)} %v_ref.1), custom_call_target="tpu_custom_call" | custom-call | tf_op jit(solution)/shard_map/pallas_call | solution.py:50
  7.2 0.0 copy-start
  7.2 62.7 %all_to_all.15.mine_ref = bf16[64,256,128]{2,1,0:T(8,128)(2,1)} all-to-all(bf16[64,256,128]{2,1,0:T(8,128)(2,1)} %bitcast.2), channel_id=1, replica_groups=mesh['near'=2,'z'=4,'core'=2,'far'=2,'y'=4] {'near','z','far','y'}, dimensions={0} | all-to-all | bytes 8388608 | tf_op jit(solution)/shard_map/all_to_all | solution.py:233
  69.9 0.0 collective-permute-start
  69.9 8.1 %all-to-all-start = ((bf16[32,128,128]{2,1,0:T(8,128)(2,1)}), bf16[32,128,128]{2,1,0:T(8,128)(2,1)S(1)}, u32[]{:S(2)}, u32[]{:S(2)}) async-start(bf16[32,128,128]{2,1,0:T(8,128)(2,1)} %get-tuple-element.7), calls=%async_computation | async-start | bytes 2097152 | tf_op jit(solution)/shard_map/all_to_all | solution.py:232
  78.0 0.0 copy-done
  78.0 0.1 copy.5
  78.1 0.1 reshape.10
  78.3 16.7 %all-to-all-done.q_ref = bf16[32,128,128]{2,1,0:T(8,128)(2,1)S(1)} async-done(((bf16[32,128,128]{2,1,0:T(8,128)(2,1)}), bf16[32,128,128]{2,1,0:T(8,128)(2,1)S(1)}, u32[]{:S(2)}, u32[]{:S(2)}) %all-to-all-start) | async-done | bytes 1048608 | tf_op jit(solution)/shard_map/all_to_all | solution.py:232
  94.9 0.0 collective-permute-done.other_ref
  94.9 31.9 %shard_map.47 = bf16[32,128,128]{2,1,0:T(8,128)(2,1)S(1)} custom-call(s32[3072]{0:T(1024)S(1)} %pad_add_fusion.place_ref, bf16[32,128,128]{2,1,0:T(8,128)(2,1)S(1)} %all-to-all-done.q_ref, bf16[64,256,128]{2,1,0:T(8,128)(2,1)} %all_to_all.15.mine_ref, bf16[64,256,128]{2,1,0:T(8,128)(2,1)} %collective-permute-done.other_ref), custom_call_target="tpu_custom_call" | custom-call | flops 6442450944 | bytes 10485760 | tf_op jit(solution)/shard_map/pallas_call | solution.py:201
  126.9 21.1 %all_to_all.16.x_ref = bf16[32,128,128]{2,1,0:T(8,128)(2,1)} all-to-all(bf16[32,128,128]{2,1,0:T(8,128)(2,1)S(1)} %shard_map.47), channel_id=1, replica_groups=mesh['near'=2,'z'=4,'core'=2,'far'=2,'y'=4] {'near','z','y'}, dimensions={0} | all-to-all | bytes 2097152 | tf_op jit(solution)/shard_map/all_to_all | solution.py:250
  147.9 5.5 %shard_map.48 = bf16[256,2048]{1,0:T(8,128)(2,1)} custom-call(bf16[32,128,128]{2,1,0:T(8,128)(2,1)} %all_to_all.16.x_ref), custom_call_target="tpu_custom_call" | custom-call | tf_op jit(solution)/shard_map/pallas_call | solution.py:76
  (3 shorter events, 0.1 us)
Async XLA Ops:
  7.2 70.8 %copy-start = (s32[256,24]{0,1:T(8,128)S(1)}, s32[256,24]{0,1:T(8,128)}, u32[]{:S(2)}) copy-start(s32[256,24]{0,1:T(8,128)} %param.7) | copy-start | bytes 73732
  69.9 25.1 %collective-permute-start = (bf16[64,256,128]{2,1,0:T(8,128)(2,1)}, bf16[64,256,128]{2,1,0:T(8,128)(2,1)}, u32[]{:S(2)}, u32[]{:S(2)}) collective-permute-start(bf16[64,256,128]{2,1,0:T(8,128)(2,1)} %all_to_all.15.mine_ref), channel_id=1, source_target_pairs={{0,8},{8,0},{1,9},{9,1},{2,10},{10,2},{3,11},{11,3},{4,12},{12,4},... | collective-permute-start | bytes 12582920 | tf_op jit(solution)/shard_map/ppermute | solution.py:234
  69.9 25.1 %all-to-all-start = ((bf16[32,128,128]{2,1,0:T(8,128)(2,1)}), bf16[32,128,128]{2,1,0:T(8,128)(2,1)S(1)}, u32[]{:S(2)}, u32[]{:S(2)}) async-start(bf16[32,128,128]{2,1,0:T(8,128)(2,1)} %get-tuple-element.7), calls=%async_computation | async-start | bytes 2097152 | tf_op jit(solution)/shard_map/all_to_all | solution.py:232

commit v4 on v3

--- a/solution.py
+++ b/solution.py
@@ -12,10 +12,11 @@
 BLOCK = 128
 ACT = 24
 LIMIT = 2.0**100
+KEY_COPIES = 4
 
 AXES = ("near", "z", "core", "far", "y")
-HEAD_AXES = ("near", "z", "y")
-CHIP_AXES = ("near", "z", "far", "y")
+HEAD_AXES = ("z", "near", "y")
+CHIP_AXES = ("z", "near", "y", "far")
 
 
 def swap_halves(x):
@@ -29,36 +30,70 @@
     return jnp.where(low, top, swap_halves(bottom)), jnp.where(low, swap_halves(top), bottom)
 
 
-def pack_kernel(q_ref, k_ref, v_ref, q_out, kv_out):
-    for pair in range(q_out.shape[0] // 2):
-        columns = pl.ds(pair * 2 * HD, 2 * HD)
-        for n, block in enumerate(both_blocks(q_ref[:, columns])):
-            q_out[2 * pair + n] = block
-        keys = both_blocks(k_ref[:, columns])
-        v = jnp.transpose(v_ref[:, columns])
-        for n in range(2):
-            rows = v[n * HD : (n + 1) * HD]
-            for copy in range(kv_out.shape[1]):
-                kv_out[0, copy, 2 * pair + n, :BLOCK] = keys[n]
-                kv_out[0, copy, 2 * pair + n, BLOCK : BLOCK + HD] = rows[:, :BLOCK]
-                kv_out[0, copy, 2 * pair + n, BLOCK + HD :] = rows[:, BLOCK:]
-
-
-def pack(queries, keys, values, groups, copies, heads):
-    rows, width = queries.shape
-    block = pl.BlockSpec((rows, width // groups), lambda g: (0, g))
+def pack_kernel(q_ref, k_ref, v_ref, q_out, kv_out, q, k, v, q_new, kv_new, came, gone):
+    heads, copies = kv_out.shape[:2]
+    parts = came.shape[0]
+    width = q.shape[1] // parts
+    share = heads // parts
+    arrivals = []
+    for part in range(parts):
+        columns = pl.ds(part * width, width)
+        arrivals.append(
+            [
+                pltpu.make_async_copy(there.at[:, columns], here.at[:, columns], came.at[part, n])
+                for n, (there, here) in enumerate(((k_ref, k), (v_ref, v), (q_ref, q)))
+            ]
+        )
+        for copy in arrivals[part]:
+            copy.start()
+    departures = []
+    for part in range(parts):
+        for copy in arrivals[part]:
+            copy.wait()
+        for pair in range(part * width // (2 * HD), (part + 1) * width // (2 * HD)):
+            columns = pl.ds(pair * 2 * HD, 2 * HD)
+            keys = both_blocks(k[:, columns])
+            queries = both_blocks(q[:, columns])
+            values = jnp.transpose(v[:, columns])
+            for n in range(2):
+                rows = values[n * HD : (n + 1) * HD]
+                q_new[2 * pair + n] = queries[n]
+                kv_new[2 * pair + n, :BLOCK] = keys[n]
+                kv_new[2 * pair + n, BLOCK : BLOCK + HD] = rows[:, :BLOCK]
+                kv_new[2 * pair + n, BLOCK + HD :] = rows[:, BLOCK:]
+        here = pl.ds(part * share, share)
+        for n in range(copies):
+            departures.append(
+                pltpu.make_async_copy(kv_new.at[here], kv_out.at[here, n], gone.at[part, n])
+            )
+        departures.append(
+            pltpu.make_async_copy(q_new.at[here], q_out.at[here], gone.at[part, copies])
+        )
+        for copy in departures[-copies - 1 :]:
+            copy.start()
+    for copy in departures:
+        copy.wait()
+
+
+def pack(queries, keys, values, heads, copies, parts):
+    anywhere = pl.BlockSpec(memory_space=pl.ANY)
+    whole = pltpu.VMEM(queries.shape, queries.dtype)
     return pl.pallas_call(
         pack_kernel,
-        grid=(groups,),
         out_shape=(
-            jax.ShapeDtypeStruct((groups * heads, BLOCK, 2 * HD), queries.dtype),
-            jax.ShapeDtypeStruct((groups, copies, heads, 2 * BLOCK, BLOCK), keys.dtype),
+            jax.ShapeDtypeStruct((heads, BLOCK, 2 * HD), queries.dtype),
+            jax.ShapeDtypeStruct((heads, copies, 2 * BLOCK, BLOCK), keys.dtype),
         ),
-        in_specs=[block] * 3,
-        out_specs=(
-            pl.BlockSpec((heads, BLOCK, 2 * HD), lambda g: (g, 0, 0)),
-            pl.BlockSpec((1, copies, heads, 2 * BLOCK, BLOCK), lambda g: (g, 0, 0, 0, 0)),
-        ),
+        in_specs=[anywhere] * 3,
+        out_specs=(anywhere, anywhere),
+        scratch_shapes=[whole] * 3
+        + [
+            pltpu.VMEM((heads, BLOCK, 2 * HD), queries.dtype),
+            pltpu.VMEM((heads, 2 * BLOCK, BLOCK), keys.dtype),
+            pltpu.SemaphoreType.DMA((parts, 3)),
+            pltpu.SemaphoreType.DMA((parts, copies + 1)),
+        ],
+        compiler_params=pltpu.CompilerParams(vmem_limit_bytes=63 * 2**20),
     )(queries, keys, values)
 
 
@@ -90,34 +125,24 @@
     low = lax.broadcasted_iota(jnp.int32, (BLOCK, BLOCK), 1) < HD
 
     keys, rest = [], []
+    piece = chunks // KEY_COPIES
     for n, ref in enumerate((mine_ref, other_ref)):
-        first, second = pl.ds(n * chunks, chunks), pl.ds((2 + n) * chunks, chunks)
-        sem = sems.at[n]
-        keys.append(pltpu.make_async_copy(ref.at[:, :BLOCK, :], kk.at[first], sem.at[0]))
-        upper, lower = ref.at[:, BLOCK : BLOCK + HD, :], ref.at[:, BLOCK + HD :, :]
-        rest.append(pltpu.make_async_copy(upper, vt.at[first], sem.at[1]))
-        rest.append(pltpu.make_async_copy(lower, vt.at[second], sem.at[2]))
-    for copy in keys + rest:
+        for part in range(KEY_COPIES):
+            there, here = pl.ds(part * piece, piece), pl.ds(n * chunks + part * piece, piece)
+            copy = pltpu.make_async_copy(
+                ref.at[there, :BLOCK, :], kk.at[here], sems.at[n, part]
+            )
+            keys.append((copy, n * chunks + part * piece))
+        for side in range(2):
+            here = pl.ds((2 * side + n) * chunks, chunks)
+            rows = ref.at[:, BLOCK + side * HD : BLOCK + (side + 1) * HD, :]
+            rest.append(
+                pltpu.make_async_copy(rows, vt.at[here], sems.at[n, KEY_COPIES + side])
+            )
+    for copy, _ in keys:
         copy.start()
-
-    for n in range(2):
-        keys[n].wait()
-
-        @pl.loop(n * chunks, (n + 1) * chunks, step=8)
-        def _(first):
-            for c in [first + u for u in range(8)]:
-                kk[2 * chunks + c] = swap_halves(kk[c])
-
-    def scores(i, t, n):
-        rows = []
-        for j in range(n):
-            a = place_ref[2 * i * ACT + t + j]
-            b = place_ref[(2 * (pairs + i) + 1) * ACT + t + j]
-            rows.append(jnp.where(low, kk[a], kk[b]))
-        rows = jnp.concatenate(rows, axis=0) if n > 1 else rows[0]
-        return jnp.dot(rows, q2[i], preferred_element_type=jnp.float32)
-
-    factor = math.log2(math.e) / math.sqrt(HD)
+    for copy in rest:
+        copy.start()
 
     @pl.loop(0, pairs, step=4)
     def _(first):
@@ -128,7 +153,29 @@
             q2[i, :HD, BLOCK:] = zero
             q2[i, HD:, :BLOCK] = zero
             q2[i, HD:, BLOCK:] = q[HD:]
-        for i in [first + u for u in range(4)]:
+
+    for copy, begin in keys:
+        copy.wait()
+
+        @pl.loop(begin, begin + piece, step=8)
+        def _(first):
+            for c in [first + u for u in range(8)]:
+                kk[2 * chunks + c] = swap_halves(kk[c])
+
+    def scores(i, t, n):
+        rows = []
+        for j in range(n):
+            a = place_ref[2 * i * ACT + t + j]
+            b = place_ref[(2 * (pairs + i) + 1) * ACT + t + j]
+            rows.append(jnp.where(low, kk[a], kk[b]))
+        rows = jnp.concatenate(rows, axis=0) if n > 1 else rows[0]
+        return jnp.dot(rows, q2[i], preferred_element_type=jnp.float32)
+
+    factor = math.log2(math.e) / math.sqrt(HD)
+
+    @pl.loop(0, pairs, step=8)
+    def _(first):
+        for i in [first + u for u in range(8)]:
             shift[i] = factor * jnp.max(scores(i, 0, 1), axis=0, keepdims=True)
 
     for copy in rest:
@@ -173,9 +220,9 @@
                 if t + count == ACT:
                     finish(i, total)
 
-    @pl.loop(0, pairs, step=4)
+    @pl.loop(0, pairs, step=8)
     def _(first):
-        run([first + u for u in range(4)], 4)
+        run([first + u for u in range(8)], 4)
 
     def lost(s):
         return jnp.max(jnp.where(s <= LIMIT, 0.0, 1.0)) > 0.0
@@ -209,7 +256,7 @@
             pltpu.VMEM((pairs, BLOCK, 2 * BLOCK), jnp.bfloat16),
             pltpu.VMEM((pairs, 1, 2 * BLOCK), jnp.float32),
             pltpu.VMEM((pairs, 1, 2 * BLOCK), jnp.float32),
-            pltpu.SemaphoreType.DMA((2, 3)),
+            pltpu.SemaphoreType.DMA((2, KEY_COPIES + 2)),
         ],
         compiler_params=pltpu.CompilerParams(vmem_limit_bytes=48 * 2**20),
         cost_estimate=pl.CostEstimate(
@@ -221,34 +268,34 @@
 
 
 def on_device(queries, keys, values, active):
-    near, z, far, y = (lax.axis_size(a) for a in CHIP_AXES)
+    z, near, y, far = (lax.axis_size(a) for a in CHIP_AXES)
     heads = near * z * y
     blocks = queries.shape[0] // BLOCK
     core, far_id = lax.axis_index("core"), lax.axis_index("far")
 
-    q, kv = pack(queries, keys, values, near * z, far, y)
-    kv = kv.reshape(near * z * far * y, 2 * BLOCK, BLOCK)
+    q, kv = pack(queries, keys, values, heads, far, 4)
+    kv = kv.reshape(heads * far, 2 * BLOCK, BLOCK)
 
     q = lax.all_to_all(q, HEAD_AXES, 0, 0, tiled=True)
     mine = lax.all_to_all(kv, CHIP_AXES, 0, 0, tiled=True)
     other = lax.ppermute(mine, "core", [(0, 1), (1, 0)])
 
-    per_core = far * y * blocks
-    chunks = near * z * far * y
-    table = active.reshape(near * z, 2, far, y, blocks, ACT)
+    chunks = heads * far
+    table = active.reshape(near, z, 2, far, y, blocks, ACT)
     table = lax.dynamic_slice(
-        table, (0, core, far_id, 0, 0, 0), (near * z, 1, 1, y, blocks, ACT)
-    ).reshape(-1)
-    of_other = ((table // per_core) % 2) != core
-    chunk = (table // (2 * per_core) * per_core + table % per_core) // 2
-    chunk = chunk + jnp.where(of_other, chunks, 0)
-    place = jnp.concatenate(
-        [chunk + 2 * chunks * (table % 2), chunk + 2 * chunks * (1 - table % 2)]
+        table, (0, 0, core, far_id, 0, 0, 0), (near, z, 1, 1, y, blocks, ACT)
     )
+    table = jnp.swapaxes(table, 0, 1).reshape(-1)
+    device, half = table // blocks, table % blocks
+    chunk = device // (y * far * 2)
+    chunk = chunk % z * near + chunk // z
+    chunk = (chunk * y + device % y) * far + device // y % far
+    chunk = chunk + jnp.where(device // (y * far) % 2 != core, chunks, 0)
+    place = jnp.concatenate([chunk + 2 * chunks * half, chunk + 2 * chunks * (1 - half)])
 
     out = attend(place, q, mine, other)
     out = lax.all_to_all(out, HEAD_AXES, 0, 0, tiled=True)
-    return unpack(out, near * z)
+    return unpack(out, 2)
 
 
 def solution(mesh):

time: 154 us -> 142 us (0.922)
  Pallas kernels: 44.6 us -> 34.4 us
  starting transfers between devices: 8.12 us -> 5.91 us
    pallas_call x1, Pallas kernels: 31.9 us -> 28.1 us  [attend(): pl.pallas_call(attend_kernel, out_shape=jax.ShapeDtypeStruct(q.shape, jnp...]
    pallas_call x1, Pallas kernels: 7.18 us -> 3.92 us  [pack(): pl.pallas_call(pack_kernel, out_shape=(jax.ShapeDtypeStruct((heads, BLOCK...]
    pallas_call x1, Pallas kernels: 5.51 us -> 2.3 us  [unpack(): pl.pallas_call(unpack_kernel, grid=(groups,), out_shape=jax.ShapeDtypeStr...]
    all_to_all x1, starting transfers between devices: 8.12 us -> 5.91 us  [on_device(): q = lax.all_to_all(q, HEAD_AXES, 0, 0, tiled=True)]
where the time goes in v4:
time: 142 us; the launch traced here: 140 us
  blocking collectives  82.8 us (58%)
  Pallas kernels  34.4 us (24%)
  waiting for transfers between devices  16.5 us (12%)
  starting transfers between devices  5.91 us (4%)
    all_to_all x1, blocking collectives, on_device(): mine = lax.all_to_all(kv, CHIP_AXES, 0, 0, tiled=True)  61.2 us
    pallas_call x1, Pallas kernels, attend(): pl.pallas_call(attend_kernel, out_shape=jax.ShapeDtypeStruct(q.shape, jnp...  28.1 us
    all_to_all x1, blocking collectives, on_device(): out = lax.all_to_all(out, HEAD_AXES, 0, 0, tiled=True)  21.6 us
    all_to_all x1, waiting for transfers between devices, on_device(): q = lax.all_to_all(q, HEAD_AXES, 0, 0, tiled=True)  16.5 us
    all_to_all x1, starting transfers between devices, on_device(): q = lax.all_to_all(q, HEAD_AXES, 0, 0, tiled=True)  5.91 us
    pallas_call x1, Pallas kernels, pack(): pl.pallas_call(pack_kernel, out_shape=(jax.ShapeDtypeStruct((heads, BLOCK...  3.92 us
  transfers between devices with their start and end apart: 2, of which 1 were waited for; matrix products, arithmetic and copies ran while one was open for 0% of the time, Pallas kernels for 0%

profile of v4, /device:TPU:6, one launch (start us, length us, event | category | flops | bytes accessed | tf_op | source)
XLA Modules:
  0.0 140.0 jit_solution(8197210387424685373)
XLA Ops:
  0.0 3.9 %shard_map.46 = (bf16[32,128,128]{2,1,0:T(8,128)(2,1)}, bf16[32,2,256,128]{3,2,1,0:T(8,128)(2,1)}) custom-call(bf16[256,2048]{1,0:T(8,128)(2,1)} %q_ref.1, bf16[256,2048]{1,0:T(8,128)(2,1)} %k_ref.1, bf16[256,2048]{1,0:T(8,128)(2,1)} %v_ref.1), custom_call_target="tpu_custom_call" | custom-call | tf_op jit(solution)/shard_map/pallas_call | solution.py:81
  3.9 0.0 copy-start
  3.9 61.2 %all_to_all.15.mine_ref = bf16[64,256,128]{2,1,0:T(8,128)(2,1)} all-to-all(bf16[64,256,128]{2,1,0:T(8,128)(2,1)} %bitcast.6), channel_id=1, replica_groups=mesh['near'=2,'z'=4,'core'=2,'far'=2,'y'=4] {'z','near','y','far'}, dimensions={0} | all-to-all | bytes 8388608 | tf_op jit(solution)/shard_map/all_to_all | solution.py:280
  65.2 0.0 collective-permute-start
  65.2 5.9 %all-to-all-start = ((bf16[32,128,128]{2,1,0:T(8,128)(2,1)}), bf16[32,128,128]{2,1,0:T(8,128)(2,1)S(1)}, u32[]{:S(2)}, u32[]{:S(2)}) async-start(bf16[32,128,128]{2,1,0:T(8,128)(2,1)} %get-tuple-element.7), calls=%async_computation | async-start | bytes 2097152 | tf_op jit(solution)/shard_map/all_to_all | solution.py:279
  71.1 0.0 copy-done
  71.1 0.1 copy.5
  71.2 0.1 reshape.10
  71.3 0.1 multiply_add_fusion.1
  71.4 16.5 %all-to-all-done.q_ref = bf16[32,128,128]{2,1,0:T(8,128)(2,1)S(1)} async-done(((bf16[32,128,128]{2,1,0:T(8,128)(2,1)}), bf16[32,128,128]{2,1,0:T(8,128)(2,1)S(1)}, u32[]{:S(2)}, u32[]{:S(2)}) %all-to-all-start) | async-done | bytes 1048608 | tf_op jit(solution)/shard_map/all_to_all | solution.py:279
  87.9 0.0 collective-permute-done.other_ref
  87.9 28.1 %shard_map.47 = bf16[32,128,128]{2,1,0:T(8,128)(2,1)S(1)} custom-call(s32[3072]{0:T(1024)S(1)} %pad_add_fusion.place_ref, bf16[32,128,128]{2,1,0:T(8,128)(2,1)S(1)} %all-to-all-done.q_ref, bf16[64,256,128]{2,1,0:T(8,128)(2,1)} %all_to_all.15.mine_ref, bf16[64,256,128]{2,1,0:T(8,128)(2,1)} %collective-permute-done.other_ref), custom_call_target="tpu_custom_call" | custom-call | flops 6442450944 | bytes 10485760 | tf_op jit(solution)/shard_map/pallas_call | solution.py:248
  116.0 21.6 %all_to_all.16.x_ref = bf16[32,128,128]{2,1,0:T(8,128)(2,1)} all-to-all(bf16[32,128,128]{2,1,0:T(8,128)(2,1)S(1)} %shard_map.47), channel_id=1, replica_groups=mesh['near'=2,'z'=4,'core'=2,'far'=2,'y'=4] {'z','near','y'}, dimensions={0} | all-to-all | bytes 2097152 | tf_op jit(solution)/shard_map/all_to_all | solution.py:297
  137.7 2.3 %shard_map.48 = bf16[256,2048]{1,0:T(8,128)(2,1)} custom-call(bf16[32,128,128]{2,1,0:T(8,128)(2,1)} %all_to_all.16.x_ref), custom_call_target="tpu_custom_call" | custom-call | tf_op jit(solution)/shard_map/pallas_call | solution.py:111
  (4 shorter events, 0.0 us)
Async XLA Ops:
  3.9 67.2 %copy-start = (s32[256,24]{0,1:T(8,128)S(1)}, s32[256,24]{0,1:T(8,128)}, u32[]{:S(2)}) copy-start(s32[256,24]{0,1:T(8,128)} %param.7) | copy-start | bytes 73732
  65.2 22.7 %collective-permute-start = (bf16[64,256,128]{2,1,0:T(8,128)(2,1)}, bf16[64,256,128]{2,1,0:T(8,128)(2,1)}, u32[]{:S(2)}, u32[]{:S(2)}) collective-permute-start(bf16[64,256,128]{2,1,0:T(8,128)(2,1)} %all_to_all.15.mine_ref), channel_id=1, source_target_pairs={{0,8},{8,0},{1,9},{9,1},{2,10},{10,2},{3,11},{11,3},{4,12},{12,4},... | collective-permute-start | bytes 12582920 | tf_op jit(solution)/shard_map/ppermute | solution.py:281
  65.2 22.7 %all-to-all-start = ((bf16[32,128,128]{2,1,0:T(8,128)(2,1)}), bf16[32,128,128]{2,1,0:T(8,128)(2,1)S(1)}, u32[]{:S(2)}, u32[]{:S(2)}) async-start(bf16[32,128,128]{2,1,0:T(8,128)(2,1)} %get-tuple-element.7), calls=%async_computation | async-start | bytes 2097152 | tf_op jit(solution)/shard_map/all_to_all | solution.py:279

commit v5 on v4

--- a/solution.py
+++ b/solution.py
@@ -220,9 +220,9 @@
                 if t + count == ACT:
                     finish(i, total)
 
-    @pl.loop(0, pairs, step=8)
+    @pl.loop(0, pairs, step=16)
     def _(first):
-        run([first + u for u in range(8)], 4)
+        run([first + u for u in range(16)], 4)
 
     def lost(s):
         return jnp.max(jnp.where(s <= LIMIT, 0.0, 1.0)) > 0.0

time: 142 us -> 141 us (level)
  no operation moved by 1% of the time
where the time goes in v5:
time: 141 us; the launch traced here: 139 us
  blocking collectives  82.8 us (59%)
  Pallas kernels  33.6 us (24%)
  waiting for transfers between devices  16.5 us (12%)
  starting transfers between devices  5.91 us (4%)
    all_to_all x1, blocking collectives, on_device(): mine = lax.all_to_all(kv, CHIP_AXES, 0, 0, tiled=True)  61.2 us
    pallas_call x1, Pallas kernels, attend(): pl.pallas_call(attend_kernel, out_shape=jax.ShapeDtypeStruct(q.shape, jnp...  27.4 us
    all_to_all x1, blocking collectives, on_device(): out = lax.all_to_all(out, HEAD_AXES, 0, 0, tiled=True)  21.6 us
    all_to_all x1, waiting for transfers between devices, on_device(): q = lax.all_to_all(q, HEAD_AXES, 0, 0, tiled=True)  16.5 us
    all_to_all x1, starting transfers between devices, on_device(): q = lax.all_to_all(q, HEAD_AXES, 0, 0, tiled=True)  5.91 us
    pallas_call x1, Pallas kernels, pack(): pl.pallas_call(pack_kernel, out_shape=(jax.ShapeDtypeStruct((heads, BLOCK...  3.92 us
  transfers between devices with their start and end apart: 2, of which 1 were waited for; matrix products, arithmetic and copies ran while one was open for 0% of the time, Pallas kernels for 0%

profile of v5, /device:TPU:6, one launch (start us, length us, event | category | flops | bytes accessed | tf_op | source)
XLA Modules:
  0.0 139.3 jit_solution(16653158541345152755)
XLA Ops:
  0.0 3.9 %shard_map.46 = (bf16[32,128,128]{2,1,0:T(8,128)(2,1)}, bf16[32,2,256,128]{3,2,1,0:T(8,128)(2,1)}) custom-call(bf16[256,2048]{1,0:T(8,128)(2,1)} %q_ref.1, bf16[256,2048]{1,0:T(8,128)(2,1)} %k_ref.1, bf16[256,2048]{1,0:T(8,128)(2,1)} %v_ref.1), custom_call_target="tpu_custom_call" | custom-call | tf_op jit(solution)/shard_map/pallas_call | solution.py:81
  3.9 0.0 copy-start
  3.9 61.2 %all_to_all.15.mine_ref = bf16[64,256,128]{2,1,0:T(8,128)(2,1)} all-to-all(bf16[64,256,128]{2,1,0:T(8,128)(2,1)} %bitcast.6), channel_id=1, replica_groups=mesh['near'=2,'z'=4,'core'=2,'far'=2,'y'=4] {'z','near','y','far'}, dimensions={0} | all-to-all | bytes 8388608 | tf_op jit(solution)/shard_map/all_to_all | solution.py:280
  65.2 0.0 collective-permute-start
  65.2 5.9 %all-to-all-start = ((bf16[32,128,128]{2,1,0:T(8,128)(2,1)}), bf16[32,128,128]{2,1,0:T(8,128)(2,1)S(1)}, u32[]{:S(2)}, u32[]{:S(2)}) async-start(bf16[32,128,128]{2,1,0:T(8,128)(2,1)} %get-tuple-element.7), calls=%async_computation | async-start | bytes 2097152 | tf_op jit(solution)/shard_map/all_to_all | solution.py:279
  71.1 0.0 copy-done
  71.1 0.1 copy.5
  71.2 0.1 reshape.10
  71.3 0.1 multiply_add_fusion.1
  71.4 16.5 %all-to-all-done.q_ref = bf16[32,128,128]{2,1,0:T(8,128)(2,1)S(1)} async-done(((bf16[32,128,128]{2,1,0:T(8,128)(2,1)}), bf16[32,128,128]{2,1,0:T(8,128)(2,1)S(1)}, u32[]{:S(2)}, u32[]{:S(2)}) %all-to-all-start) | async-done | bytes 1048608 | tf_op jit(solution)/shard_map/all_to_all | solution.py:279
  87.9 0.0 collective-permute-done.other_ref
  87.9 27.4 %shard_map.47 = bf16[32,128,128]{2,1,0:T(8,128)(2,1)S(1)} custom-call(s32[3072]{0:T(1024)S(1)} %pad_add_fusion.place_ref, bf16[32,128,128]{2,1,0:T(8,128)(2,1)S(1)} %all-to-all-done.q_ref, bf16[64,256,128]{2,1,0:T(8,128)(2,1)} %all_to_all.15.mine_ref, bf16[64,256,128]{2,1,0:T(8,128)(2,1)} %collective-permute-done.other_ref), custom_call_target="tpu_custom_call" | custom-call | flops 6442450944 | bytes 10485760 | tf_op jit(solution)/shard_map/pallas_call | solution.py:248
  115.3 21.6 %all_to_all.16.x_ref = bf16[32,128,128]{2,1,0:T(8,128)(2,1)} all-to-all(bf16[32,128,128]{2,1,0:T(8,128)(2,1)S(1)} %shard_map.47), channel_id=1, replica_groups=mesh['near'=2,'z'=4,'core'=2,'far'=2,'y'=4] {'z','near','y'}, dimensions={0} | all-to-all | bytes 2097152 | tf_op jit(solution)/shard_map/all_to_all | solution.py:297
  137.0 2.3 %shard_map.48 = bf16[256,2048]{1,0:T(8,128)(2,1)} custom-call(bf16[32,128,128]{2,1,0:T(8,128)(2,1)} %all_to_all.16.x_ref), custom_call_target="tpu_custom_call" | custom-call | tf_op jit(solution)/shard_map/pallas_call | solution.py:111
  (4 shorter events, 0.0 us)
Async XLA Ops:
  3.9 67.2 %copy-start = (s32[256,24]{0,1:T(8,128)S(1)}, s32[256,24]{0,1:T(8,128)}, u32[]{:S(2)}) copy-start(s32[256,24]{0,1:T(8,128)} %param.7) | copy-start | bytes 73732
  65.2 22.7 %collective-permute-start = (bf16[64,256,128]{2,1,0:T(8,128)(2,1)}, bf16[64,256,128]{2,1,0:T(8,128)(2,1)}, u32[]{:S(2)}, u32[]{:S(2)}) collective-permute-start(bf16[64,256,128]{2,1,0:T(8,128)(2,1)} %all_to_all.15.mine_ref), channel_id=1, source_target_pairs={{0,8},{8,0},{1,9},{9,1},{2,10},{10,2},{3,11},{11,3},{4,12},{12,4},... | collective-permute-start | bytes 12582920 | tf_op jit(solution)/shard_map/ppermute | solution.py:281
  65.2 22.7 %all-to-all-start = ((bf16[32,128,128]{2,1,0:T(8,128)(2,1)}), bf16[32,128,128]{2,1,0:T(8,128)(2,1)S(1)}, u32[]{:S(2)}, u32[]{:S(2)}) async-start(bf16[32,128,128]{2,1,0:T(8,128)(2,1)} %get-tuple-element.7), calls=%async_computation | async-start | bytes 2097152 | tf_op jit(solution)/shard_map/all_to_all | solution.py:279

commit v6 on v5

--- a/solution.py
+++ b/solution.py
@@ -15,8 +15,8 @@
 KEY_COPIES = 4
 
 AXES = ("near", "z", "core", "far", "y")
-HEAD_AXES = ("z", "near", "y")
-CHIP_AXES = ("z", "near", "y", "far")
+HEAD_AXES = ("near", "z", "y")
+CHIP_AXES = ("near", "z", "y", "far")
 
 
 def swap_halves(x):
@@ -144,9 +144,9 @@
     for copy in rest:
         copy.start()
 
-    @pl.loop(0, pairs, step=4)
+    @pl.loop(0, pairs, step=8)
     def _(first):
-        for i in [first + u for u in range(4)]:
+        for i in [first + u for u in range(8)]:
             q = jnp.transpose(q_ref[i].astype(jnp.float32)).astype(jnp.bfloat16)
             zero = jnp.zeros((HD, BLOCK), jnp.bfloat16)
             q2[i, :HD, :BLOCK] = q[:HD]
@@ -173,9 +173,9 @@
 
     factor = math.log2(math.e) / math.sqrt(HD)
 
-    @pl.loop(0, pairs, step=8)
+    @pl.loop(0, pairs, step=16)
     def _(first):
-        for i in [first + u for u in range(8)]:
+        for i in [first + u for u in range(16)]:
             shift[i] = factor * jnp.max(scores(i, 0, 1), axis=0, keepdims=True)
 
     for copy in rest:
@@ -268,7 +268,7 @@
 
 
 def on_device(queries, keys, values, active):
-    z, near, y, far = (lax.axis_size(a) for a in CHIP_AXES)
+    near, z, y, far = (lax.axis_size(a) for a in CHIP_AXES)
     heads = near * z * y
     blocks = queries.shape[0] // BLOCK
     core, far_id = lax.axis_index("core"), lax.axis_index("far")
@@ -284,12 +284,9 @@
     table = active.reshape(near, z, 2, far, y, blocks, ACT)
     table = lax.dynamic_slice(
         table, (0, 0, core, far_id, 0, 0, 0), (near, z, 1, 1, y, blocks, ACT)
-    )
-    table = jnp.swapaxes(table, 0, 1).reshape(-1)
+    ).reshape(-1)
     device, half = table // blocks, table % blocks
-    chunk = device // (y * far * 2)
-    chunk = chunk % z * near + chunk // z
-    chunk = (chunk * y + device % y) * far + device // y % far
+    chunk = (device // (y * far * 2) * y + device % y) * far + device // y % far
     chunk = chunk + jnp.where(device // (y * far) % 2 != core, chunks, 0)
     place = jnp.concatenate([chunk + 2 * chunks * half, chunk + 2 * chunks * (1 - half)])
 

time: 141 us -> 140 us (level)
  no operation moved by 1% of the time
where the time goes in v6:
time: 140 us; the launch traced here: 138 us
  blocking collectives  83.5 us (60%)
  Pallas kernels  33.3 us (24%)
  waiting for transfers between devices  16.6 us (12%)
  starting transfers between devices  4.51 us (3%)
    all_to_all x1, blocking collectives, on_device(): mine = lax.all_to_all(kv, CHIP_AXES, 0, 0, tiled=True)  62.4 us
    pallas_call x1, Pallas kernels, attend(): pl.pallas_call(attend_kernel, out_shape=jax.ShapeDtypeStruct(q.shape, jnp...  27.1 us
    all_to_all x1, blocking collectives, on_device(): out = lax.all_to_all(out, HEAD_AXES, 0, 0, tiled=True)  21.1 us
    all_to_all x1, waiting for transfers between devices, on_device(): q = lax.all_to_all(q, HEAD_AXES, 0, 0, tiled=True)  16.6 us
    all_to_all x1, starting transfers between devices, on_device(): q = lax.all_to_all(q, HEAD_AXES, 0, 0, tiled=True)  4.5 us
    pallas_call x1, Pallas kernels, pack(): pl.pallas_call(pack_kernel, out_shape=(jax.ShapeDtypeStruct((heads, BLOCK...  3.92 us
  transfers between devices with their start and end apart: 2, of which 1 were waited for; matrix products, arithmetic and copies ran while one was open for 0% of the time, Pallas kernels for 0%

profile of v6, /device:TPU:6, one launch (start us, length us, event | category | flops | bytes accessed | tf_op | source)
XLA Modules:
  0.0 138.3 jit_solution(5678551655973298985)
XLA Ops:
  0.0 3.9 %shard_map.46 = (bf16[32,128,128]{2,1,0:T(8,128)(2,1)}, bf16[32,2,256,128]{3,2,1,0:T(8,128)(2,1)}) custom-call(bf16[256,2048]{1,0:T(8,128)(2,1)} %q_ref.1, bf16[256,2048]{1,0:T(8,128)(2,1)} %k_ref.1, bf16[256,2048]{1,0:T(8,128)(2,1)} %v_ref.1), custom_call_target="tpu_custom_call" | custom-call | tf_op jit(solution)/shard_map/pallas_call | solution.py:81
  3.9 0.0 copy-start
  3.9 62.4 %all_to_all.15.mine_ref = bf16[64,256,128]{2,1,0:T(8,128)(2,1)} all-to-all(bf16[64,256,128]{2,1,0:T(8,128)(2,1)} %bitcast.2), channel_id=1, replica_groups=mesh['near'=2,'z'=4,'core'=2,'far'=2,'y'=4] {'near','z','y','far'}, dimensions={0} | all-to-all | bytes 8388608 | tf_op jit(solution)/shard_map/all_to_all | solution.py:280
  66.4 0.0 collective-permute-start
  66.4 4.5 %all-to-all-start = ((bf16[32,128,128]{2,1,0:T(8,128)(2,1)}), bf16[32,128,128]{2,1,0:T(8,128)(2,1)S(1)}, u32[]{:S(2)}, u32[]{:S(2)}) async-start(bf16[32,128,128]{2,1,0:T(8,128)(2,1)} %get-tuple-element.7), calls=%async_computation | async-start | bytes 2097152 | tf_op jit(solution)/shard_map/all_to_all | solution.py:279
  70.9 0.0 copy-done
  70.9 0.1 copy.5
  71.0 0.1 reshape.10
  71.2 16.6 %all-to-all-done.q_ref = bf16[32,128,128]{2,1,0:T(8,128)(2,1)S(1)} async-done(((bf16[32,128,128]{2,1,0:T(8,128)(2,1)}), bf16[32,128,128]{2,1,0:T(8,128)(2,1)S(1)}, u32[]{:S(2)}, u32[]{:S(2)}) %all-to-all-start) | async-done | bytes 1048608 | tf_op jit(solution)/shard_map/all_to_all | solution.py:279
  87.8 0.0 collective-permute-done.other_ref
  87.8 27.1 %shard_map.47 = bf16[32,128,128]{2,1,0:T(8,128)(2,1)S(1)} custom-call(s32[3072]{0:T(1024)S(1)} %pad_add_fusion.place_ref, bf16[32,128,128]{2,1,0:T(8,128)(2,1)S(1)} %all-to-all-done.q_ref, bf16[64,256,128]{2,1,0:T(8,128)(2,1)} %all_to_all.15.mine_ref, bf16[64,256,128]{2,1,0:T(8,128)(2,1)} %collective-permute-done.other_ref), custom_call_target="tpu_custom_call" | custom-call | flops 6442450944 | bytes 10485760 | tf_op jit(solution)/shard_map/pallas_call | solution.py:248
  115.0 21.1 %all_to_all.16.x_ref = bf16[32,128,128]{2,1,0:T(8,128)(2,1)} all-to-all(bf16[32,128,128]{2,1,0:T(8,128)(2,1)S(1)} %shard_map.47), channel_id=1, replica_groups=mesh['near'=2,'z'=4,'core'=2,'far'=2,'y'=4] {'near','z','y'}, dimensions={0} | all-to-all | bytes 2097152 | tf_op jit(solution)/shard_map/all_to_all | solution.py:294
  136.0 2.3 %shard_map.48 = bf16[256,2048]{1,0:T(8,128)(2,1)} custom-call(bf16[32,128,128]{2,1,0:T(8,128)(2,1)} %all_to_all.16.x_ref), custom_call_target="tpu_custom_call" | custom-call | tf_op jit(solution)/shard_map/pallas_call | solution.py:111
  (4 shorter events, 0.1 us)
Async XLA Ops:
  3.9 67.0 %copy-start = (s32[256,24]{0,1:T(8,128)S(1)}, s32[256,24]{0,1:T(8,128)}, u32[]{:S(2)}) copy-start(s32[256,24]{0,1:T(8,128)} %param.7) | copy-start | bytes 73732
  66.4 21.5 %collective-permute-start = (bf16[64,256,128]{2,1,0:T(8,128)(2,1)}, bf16[64,256,128]{2,1,0:T(8,128)(2,1)}, u32[]{:S(2)}, u32[]{:S(2)}) collective-permute-start(bf16[64,256,128]{2,1,0:T(8,128)(2,1)} %all_to_all.15.mine_ref), channel_id=1, source_target_pairs={{0,8},{8,0},{1,9},{9,1},{2,10},{10,2},{3,11},{11,3},{4,12},{12,4},... | collective-permute-start | bytes 12582920 | tf_op jit(solution)/shard_map/ppermute | solution.py:281
  66.4 21.5 %all-to-all-start = ((bf16[32,128,128]{2,1,0:T(8,128)(2,1)}), bf16[32,128,128]{2,1,0:T(8,128)(2,1)S(1)}, u32[]{:S(2)}, u32[]{:S(2)}) async-start(bf16[32,128,128]{2,1,0:T(8,128)(2,1)} %get-tuple-element.7), calls=%async_computation | async-start | bytes 2097152 | tf_op jit(solution)/shard_map/all_to_all | solution.py:279

commit v7 on v6

--- a/solution.py
+++ b/solution.py
@@ -220,9 +220,7 @@
                 if t + count == ACT:
                     finish(i, total)
 
-    @pl.loop(0, pairs, step=16)
-    def _(first):
-        run([first + u for u in range(16)], 4)
+    run(range(pairs), 4)
 
     def lost(s):
         return jnp.max(jnp.where(s <= LIMIT, 0.0, 1.0)) > 0.0

time: 140 us -> 140 us (level)
  no operation moved by 1% of the time
where the time goes in v7:
time: 140 us; the launch traced here: 139 us
  blocking collectives  83.5 us (60%)
  Pallas kernels  33.8 us (24%)
  waiting for transfers between devices  16.6 us (12%)
  starting transfers between devices  4.51 us (3%)
    all_to_all x1, blocking collectives, on_device(): mine = lax.all_to_all(kv, CHIP_AXES, 0, 0, tiled=True)  62.4 us
    pallas_call x1, Pallas kernels, attend(): pl.pallas_call(attend_kernel, out_shape=jax.ShapeDtypeStruct(q.shape, jnp...  27.6 us
    all_to_all x1, blocking collectives, on_device(): out = lax.all_to_all(out, HEAD_AXES, 0, 0, tiled=True)  21.1 us
    all_to_all x1, waiting for transfers between devices, on_device(): q = lax.all_to_all(q, HEAD_AXES, 0, 0, tiled=True)  16.6 us
    all_to_all x1, starting transfers between devices, on_device(): q = lax.all_to_all(q, HEAD_AXES, 0, 0, tiled=True)  4.5 us
    pallas_call x1, Pallas kernels, pack(): pl.pallas_call(pack_kernel, out_shape=(jax.ShapeDtypeStruct((heads, BLOCK...  3.92 us
  transfers between devices with their start and end apart: 2, of which 1 were waited for; matrix products, arithmetic and copies ran while one was open for 0% of the time, Pallas kernels for 0%

profile of v7, /device:TPU:6, one launch (start us, length us, event | category | flops | bytes accessed | tf_op | source)
XLA Modules:
  0.0 138.8 jit_solution(5033042121775609487)
XLA Ops:
  0.0 3.9 %shard_map.46 = (bf16[32,128,128]{2,1,0:T(8,128)(2,1)}, bf16[32,2,256,128]{3,2,1,0:T(8,128)(2,1)}) custom-call(bf16[256,2048]{1,0:T(8,128)(2,1)} %q_ref.1, bf16[256,2048]{1,0:T(8,128)(2,1)} %k_ref.1, bf16[256,2048]{1,0:T(8,128)(2,1)} %v_ref.1), custom_call_target="tpu_custom_call" | custom-call | tf_op jit(solution)/shard_map/pallas_call | solution.py:81
  3.9 0.0 copy-start
  3.9 62.4 %all_to_all.15.mine_ref = bf16[64,256,128]{2,1,0:T(8,128)(2,1)} all-to-all(bf16[64,256,128]{2,1,0:T(8,128)(2,1)} %bitcast.2), channel_id=1, replica_groups=mesh['near'=2,'z'=4,'core'=2,'far'=2,'y'=4] {'near','z','y','far'}, dimensions={0} | all-to-all | bytes 8388608 | tf_op jit(solution)/shard_map/all_to_all | solution.py:278
  66.4 0.0 collective-permute-start
  66.4 4.5 %all-to-all-start = ((bf16[32,128,128]{2,1,0:T(8,128)(2,1)}), bf16[32,128,128]{2,1,0:T(8,128)(2,1)S(1)}, u32[]{:S(2)}, u32[]{:S(2)}) async-start(bf16[32,128,128]{2,1,0:T(8,128)(2,1)} %get-tuple-element.7), calls=%async_computation | async-start | bytes 2097152 | tf_op jit(solution)/shard_map/all_to_all | solution.py:277
  70.9 0.0 copy-done
  70.9 0.1 copy.5
  71.0 0.1 reshape.10
  71.2 16.6 %all-to-all-done.q_ref = bf16[32,128,128]{2,1,0:T(8,128)(2,1)S(1)} async-done(((bf16[32,128,128]{2,1,0:T(8,128)(2,1)}), bf16[32,128,128]{2,1,0:T(8,128)(2,1)S(1)}, u32[]{:S(2)}, u32[]{:S(2)}) %all-to-all-start) | async-done | bytes 1048608 | tf_op jit(solution)/shard_map/all_to_all | solution.py:277
  87.8 0.0 collective-permute-done.other_ref
  87.8 27.6 %shard_map.47 = bf16[32,128,128]{2,1,0:T(8,128)(2,1)S(1)} custom-call(s32[3072]{0:T(1024)S(1)} %pad_add_fusion.place_ref, bf16[32,128,128]{2,1,0:T(8,128)(2,1)S(1)} %all-to-all-done.q_ref, bf16[64,256,128]{2,1,0:T(8,128)(2,1)} %all_to_all.15.mine_ref, bf16[64,256,128]{2,1,0:T(8,128)(2,1)} %collective-permute-done.other_ref), custom_call_target="tpu_custom_call" | custom-call | flops 6442450944 | bytes 10485760 | tf_op jit(solution)/shard_map/pallas_call | solution.py:246
  115.4 21.1 %all_to_all.16.x_ref = bf16[32,128,128]{2,1,0:T(8,128)(2,1)} all-to-all(bf16[32,128,128]{2,1,0:T(8,128)(2,1)S(1)} %shard_map.47), channel_id=1, replica_groups=mesh['near'=2,'z'=4,'core'=2,'far'=2,'y'=4] {'near','z','y'}, dimensions={0} | all-to-all | bytes 2097152 | tf_op jit(solution)/shard_map/all_to_all | solution.py:292
  136.5 2.3 %shard_map.48 = bf16[256,2048]{1,0:T(8,128)(2,1)} custom-call(bf16[32,128,128]{2,1,0:T(8,128)(2,1)} %all_to_all.16.x_ref), custom_call_target="tpu_custom_call" | custom-call | tf_op jit(solution)/shard_map/pallas_call | solution.py:111
  (4 shorter events, 0.1 us)
Async XLA Ops:
  3.9 67.0 %copy-start = (s32[256,24]{0,1:T(8,128)S(1)}, s32[256,24]{0,1:T(8,128)}, u32[]{:S(2)}) copy-start(s32[256,24]{0,1:T(8,128)} %param.7) | copy-start | bytes 73732
  66.4 21.5 %collective-permute-start = (bf16[64,256,128]{2,1,0:T(8,128)(2,1)}, bf16[64,256,128]{2,1,0:T(8,128)(2,1)}, u32[]{:S(2)}, u32[]{:S(2)}) collective-permute-start(bf16[64,256,128]{2,1,0:T(8,128)(2,1)} %all_to_all.15.mine_ref), channel_id=1, source_target_pairs={{0,8},{8,0},{1,9},{9,1},{2,10},{10,2},{3,11},{11,3},{4,12},{12,4},... | collective-permute-start | bytes 12582920 | tf_op jit(solution)/shard_map/ppermute | solution.py:279
  66.4 21.5 %all-to-all-start = ((bf16[32,128,128]{2,1,0:T(8,128)(2,1)}), bf16[32,128,128]{2,1,0:T(8,128)(2,1)S(1)}, u32[]{:S(2)}, u32[]{:S(2)}) async-start(bf16[32,128,128]{2,1,0:T(8,128)(2,1)} %get-tuple-element.7), calls=%async_computation | async-start | bytes 2097152 | tf_op jit(solution)/shard_map/all_to_all | solution.py:277
